TPU v7x, 128 devices: a whole 4x4x4 slice. The times are simulated.
128 devices in a mesh: grid: 32 (over z, x, core), lev: 4 (over y).
Axes of the slice: x: 4, y: 4, z: 4, core: 2. Of those that a mesh axis runs over, the one named last changes fastest.
Arguments:
- tiles: bfloat16 [8192, 48, 144], P('grid'), may hold values from 0 to 1
- farm_area: int32 [8192], P('grid'), may hold values from 0 to 511, as said below
- capacity: int32 [8192], P('grid'), may hold values from 20 to 200
- offsets: int32 [512], P('grid'), may hold values from 1 to 12
- state: bfloat16 [48, 8, 262144], P(None, 'lev', 'grid'), may hold values from -6 to 6
Outputs:
- sensitivity: bfloat16 [512, 8, 262144], P(None, 'lev', 'grid')
Inputs may be any that keep to these rules, and one draw needn't show every extreme that they name: `farm_area`: among the 256 farms of one grid index (aligned blocks of farms), at most 16 lie in areas of one owner, the owner of area a being a // 16; one owner, drawn from the seed, has exactly 16 farms from every grid index.
All inputs are finite; a program needn't handle non-finite values.
Results may differ from a plain program's by a relative error of at most 0.0056.
Values may be sent and summed in bfloat16 or wider, within the bound.
A program may use at most 128 MiB of HBM per device.

v0:
```python
import jax
import jax.numpy as jnp
from jax import lax
from jax.sharding import PartitionSpec as P

WMAX = 12


capacity_floor = 200.0
spread_floor = 0.05


def body(tiles, farm_area, capacity, offsets, state):
    farm_count = tiles.shape[0]
    owners = lax.axis_size("grid")
    area_count = offsets.shape[0]
    members = state.shape[0]
    steps = tiles.shape[2]
    slots = max(2, 2 * farm_count // owners)
    owner = farm_area // area_count
    local = farm_area % area_count
    order = jnp.arange(farm_count, dtype=jnp.int32)
    earlier = (owner[:, None] == owner[None, :]) & (order[None, :] < order[:, None])
    rank = jnp.sum(earlier.astype(jnp.int32), axis=1)
    target = owner * slots + rank
    slot_ids = jnp.arange(owners * slots, dtype=jnp.int32)
    placing = (slot_ids[:, None] == target[None, :]).astype(jnp.bfloat16)
    flat_used = tiles.reshape(farm_count, members * steps)
    outgoing = jnp.dot(placing, flat_used, preferred_element_type=jnp.float32).astype(jnp.bfloat16)
    labels = jnp.stack([local + 1, capacity], axis=1).astype(jnp.bfloat16)
    out_labels = jnp.dot(placing, labels, preferred_element_type=jnp.float32).astype(jnp.bfloat16)
    incoming, in_labels = (
        lax.all_to_all(
            outgoing.reshape(owners, slots, members * steps),
            "grid",
            split_axis=0,
            concat_axis=0,
            tiled=True,
        ),
        lax.all_to_all(
            out_labels.reshape(owners, slots, 2), "grid", split_axis=0, concat_axis=0, tiled=True
        ),
    )
    incoming = incoming.reshape(owners * slots, members * steps)
    in_labels = in_labels.reshape(owners * slots, 2)
    area_ids = jnp.arange(1, area_count + 1, dtype=jnp.float32)
    matches = in_labels[:, 0].astype(jnp.float32)[None, :] == area_ids[:, None]
    weights = jnp.where(matches, in_labels[:, 1][None, :], jnp.zeros((), jnp.bfloat16))
    summed = jnp.dot(weights, incoming, preferred_element_type=jnp.float32)
    total = jnp.sum(weights.astype(jnp.float32), axis=1)
    power = (summed / jnp.maximum(total, capacity_floor)[:, None]).reshape(
        area_count, members, steps
    )
    ramp_count = steps - WMAX
    times = jnp.arange(ramp_count, dtype=jnp.int32)
    step_ids = jnp.arange(steps, dtype=jnp.int32)
    later_idx = times[None, :] + offsets[:, None]
    shifting = (step_ids[None, :, None] == later_idx[:, None, :]).astype(jnp.float32)
    later = jnp.einsum("amt,ats->ams", power, shifting, precision=lax.Precision.HIGHEST)
    metric = jnp.max(later - power[:, :, :ramp_count], axis=2)
    anomaly = metric - jnp.mean(metric, axis=1, keepdims=True)
    spread = jnp.sqrt(jnp.sum(anomaly * anomaly, axis=1) / (members - 1))
    scores = (anomaly / jnp.maximum(spread, spread_floor)[:, None]).astype(jnp.bfloat16).T
    wide = state.astype(jnp.float32)
    slab = (wide - jnp.mean(wide, axis=0, keepdims=True)).astype(jnp.bfloat16)
    slab = slab.reshape(members, state.shape[1] * state.shape[2])
    product = lax.dot_general(
        lax.all_gather(scores, "grid", axis=1, tiled=True),
        slab,
        (((0,), (0,)), ((), ())),
        preferred_element_type=jnp.float32,
    )
    result = (product / (members - 1)).astype(jnp.bfloat16)
    return result.reshape(result.shape[0], state.shape[1], state.shape[2])


def solution(mesh):
    in_specs = (P("grid", None, None), P("grid"), P("grid"), P("grid"), P(None, "lev", "grid"))
    out_specs = P(None, "lev", "grid")
    return jax.shard_map(body, mesh=mesh, in_specs=in_specs, out_specs=out_specs, check_vma=False)
```

profile of v0, /device:TPU:1, one launch (start us, length us, event | category | flops | bytes accessed | tf_op | source)
XLA Modules:
  0.0 189.3 jit_solution(2081809932252789965)
XLA Ops:
  0.0 0.0 copy-start
  0.0 0.8 convert.10
  0.8 0.9 fusion.17
  1.7 0.2 convert_reduce_fusion.1
  1.9 0.0 copy-start.1
  1.9 0.6 copy-done.1
  2.5 0.8 convolution_convert_fusion.1
  3.3 0.8 reshape.72
  4.0 0.6 copy.8
  4.7 9.4 %all-to-all-start = ((bf16[32,16,2]{1,2,0:T(2,128)(2,1)}), bf16[32,16,2]{1,2,0:T(2,128)(2,1)S(1)}, u32[]{:S(2)}, u32[]{:S(2)}) async-start(bf16[32,16,2]{1,2,0:T(2,128)(2,1)} %copy.8), calls=%async_computation | async-start | bytes 32768 | tf_op jit(solution)/shard_map/all_to_all | solution.py:40
  14.1 0.0 copy-done
  14.1 5.7 %convolution_convert_fusion = bf16[512,6912]{1,0:T(8,128)(2,1)} fusion(bf16[256,6912]{0,1:T(8,128)(2,1)S(1)} %bitcast.17, s32[256]{0:T(256)} %copy-done.1), kind=kOutput, calls=%fused_computation.1 | convolution fusion | flops 1815609344 | bytes 10617856 | tf_op jit(solution)/shard_map/dot_general | solution.py:29
  19.8 1.3 all-to-all-done
  21.0 6.2 %all-to-all-start.1 = ((bf16[32,16,6912]{2,1,0:T(8,128)(2,1)}), bf16[32,16,6912]{2,1,0:T(8,128)(2,1)}, u32[]{:S(2)}, u32[]{:S(2)}) async-start(bf16[32,16,6912]{2,1,0:T(8,128)(2,1)} %bitcast.18), calls=%async_computation.1 | async-start | bytes 14155776 | tf_op jit(solution)/shard_map/all_to_all | solution.py:33
  27.2 2.7 %convert_reduce_fusion = f32[2,8192]{1,0:T(2,128)S(1)} fusion(bf16[48,2,8192]{2,1,0:T(2,128)(2,1)} %param.9), kind=kLoop, calls=%fused_computation.4 | loop fusion | flops 1556480 | bytes 1638400 | tf_op jit(solution)/shard_map/reduce_sum | solution.py:65
  29.9 0.0 copy-start.2
  30.0 3.1 %fusion = bf16[48,2,8192]{2,1,0:T(2,128)(2,1)S(1)} fusion(bf16[48,2,8192]{2,1,0:T(2,128)(2,1)} %param.9, f32[2,8192]{1,0:T(2,128)S(1)} %broadcast_multiply_fusion), kind=kLoop, calls=%fused_computation.5 | loop fusion | flops 2359296 | bytes 3211264 | tf_op jit(solution)/shard_map/convert_element_type | solution.py:65
  33.0 2.0 %copy.10 = bf16[6,8,2,8192]{3,1,2,0:T(8,128)(2,1)} copy(bf16[6,8,2,8192]{3,2,1,0:T(2,128)(2,1)S(1)} %bitcast.20) | data formatting | bytes 3145728
  35.1 0.5 iota_add_fusion.1
  35.5 0.0 copy-done.2
  35.5 0.7 iota_add_fusion
  36.2 0.6 copy.9
  36.8 0.8 reshape.73
  37.6 0.8 convert_reduce_fusion.2
  38.4 72.3 %all-to-all-done.1 = bf16[32,16,6912]{2,1,0:T(8,128)(2,1)} async-done(((bf16[32,16,6912]{2,1,0:T(8,128)(2,1)}), bf16[32,16,6912]{2,1,0:T(8,128)(2,1)}, u32[]{:S(2)}, u32[]{:S(2)}) %all-to-all-start.1) | async-done | bytes 7077920 | tf_op jit(solution)/shard_map/all_to_all | solution.py:33
  110.7 4.9 %convolution_divide_fusion = f32[16,6912]{1,0:T(8,128)} fusion(bf16[512,6912]{1,0:T(8,128)(2,1)} %bitcast.3, f32[16]{0:T(128)S(1)} %broadcast_maximum_fusion, f32[512]{0:T(512)S(1)} %bitcast.22, f32[16]{0:T(128)} %iota_add_fusion.1, bf16[512]{0:T(512)(128)(2,1)S(1)} %get-tuple-element.5), kind=kOutput, calls=%fused_computation.2 | convolution fusion | flops 113373184 | bytes 7523456 | tf_op jit(solution)/shard_map/dot_general | solution.py:49
  115.6 2.5 %reshape.77 = f32[16,48,144]{2,1,0:T(8,128)} reshape(f32[16,6912]{1,0:T(8,128)} %convolution_divide_fusion) | data formatting | bytes 884736 | tf_op jit(solution)/shard_map/reshape | solution.py:51
  118.1 2.9 %fusion.3 = f32[16,48]{1,0:T(8,128)S(1)} fusion(f32[16,48,144]{2,1,0:T(8,128)} %reshape.77, s32[16,132]{1,0:T(8,128)} %iota_add_fusion), kind=kOutput, calls=%fused_computation.9 | convolution fusion | flops 175683840 | bytes 1592320 | tf_op jit(solution)/shard_map/amt,ats->ams/dot_general | solution.py:59
  121.0 0.1 reduce_sum.47
  121.1 0.2 multiply_reduce_fusion
  121.3 0.1 fusion.12
  121.4 28.4 %all_gather.3 = bf16[48,512]{0,1:T(8,128)(2,1)} all-gather(bf16[48,16]{0,1:T(8,128)(2,1)S(1)} %fusion.12), channel_id=1, replica_groups=mesh['grid'=32,'lev'=4] {'grid'}, dimensions={1}, use_global_device_ids=true | all-gather | bytes 50688 | tf_op jit(solution)/shard_map/all_gather | solution.py:68
  149.8 11.7 %multiply_convert_fusion = bf16[512,16384]{1,0:T(8,128)(2,1)} fusion(bf16[48,512]{0,1:T(8,128)(2,1)} %all_gather.3, bf16[48,16384]{1,0:T(8,128)(2,1)} %bitcast.19), kind=kOutput, calls=%fused_computation | convolution fusion | flops 822083584 | bytes 18399232 | tf_op jit(solution)/shard_map/dot_general | solution.py:67
  161.5 27.7 %reshape.79 = bf16[512,2,8192]{2,1,0:T(2,128)(2,1)} reshape(bf16[512,16384]{1,0:T(8,128)(2,1)} %multiply_convert_fusion) | data formatting | bytes 33554432 | tf_op jit(solution)/shard_map/reshape | solution.py:74
  (8 shorter events, 0.1 us)
Async XLA Ops:
  0.0 14.1 %copy-start = (bf16[256,48,144]{0,2,1:T(8,128)(2,1)S(1)}, bf16[256,48,144]{0,2,1:T(8,128)(2,1)}, u32[]{:S(2)}) copy-start(bf16[256,48,144]{0,2,1:T(8,128)(2,1)} %param.5) | copy-start | bytes 10616836
  1.9 0.6 copy-start.1
  4.7 16.4 %all-to-all-start = ((bf16[32,16,2]{1,2,0:T(2,128)(2,1)}), bf16[32,16,2]{1,2,0:T(2,128)(2,1)S(1)}, u32[]{:S(2)}, u32[]{:S(2)}) async-start(bf16[32,16,2]{1,2,0:T(2,128)(2,1)} %copy.8), calls=%async_computation | async-start | bytes 32768 | tf_op jit(solution)/shard_map/all_to_all | solution.py:40
  21.0 89.7 %all-to-all-start.1 = ((bf16[32,16,6912]{2,1,0:T(8,128)(2,1)}), bf16[32,16,6912]{2,1,0:T(8,128)(2,1)}, u32[]{:S(2)}, u32[]{:S(2)}) async-start(bf16[32,16,6912]{2,1,0:T(8,128)(2,1)} %bitcast.18), calls=%async_computation.1 | async-start | bytes 14155776 | tf_op jit(solution)/shard_map/all_to_all | solution.py:33
  29.9 5.6 %copy-start.2 = (s32[16]{0:T(128)S(1)}, s32[16]{0:T(128)}, u32[]{:S(2)}) copy-start(s32[16]{0:T(128)} %param.8) | copy-start | bytes 196
where the time goes:
time: 191 us; the launch traced here: 189 us
  waiting for transfers between devices  73.6 us (39%)
  local copies, waits for them, and re-layouts  35.6 us (19%)
  blocking collectives  28.4 us (15%)
  matrix products  25.9 us (14%)
  starting transfers between devices  15.6 us (8%)
  other arithmetic  10 us (5%)
    all_to_all x1, waiting for transfers between devices, body(): lax.all_to_all(outgoing.reshape(owners, slots, members * steps), 'grid',...  72.3 us
    all_gather x1, blocking collectives, body(): lax.all_gather(scores, 'grid', axis=1, tiled=True)  28.4 us
    reshape x1, local copies, waits for them, and re-layouts, body(): return result.reshape(result.shape[0], state.shape[1], state.shape[2])  27.7 us
    dot_general x1, matrix products, body(): lax.dot_general(lax.all_gather(scores, 'grid', axis=1, tiled=True), slab,...  11.7 us
    all_to_all x1, starting transfers between devices, body(): lax.all_to_all(out_labels.reshape(owners, slots, 2), 'grid', split_axis=0...  9.43 us
    all_to_all x1, starting transfers between devices, body(): lax.all_to_all(outgoing.reshape(owners, slots, members * steps), 'grid',...  6.16 us
    dot_general x1, matrix products, body(): jnp.dot(placing, flat_used, preferred_element_type=jnp.float32)  5.66 us
    dot_general x1, matrix products, body(): summed = jnp.dot(weights, incoming, preferred_element_type=jnp.float32)  4.86 us
  transfers between devices with their start and end apart: 2, of which 2 were waited for; matrix products, arithmetic and copies ran while one was open for 9% of the time, Pallas kernels for 0%

commit v1 on v0

v1 whole, which is shorter than its diff:
```python
import jax
import jax.numpy as jnp
from jax import lax
from jax.experimental import pallas as pl
from jax.experimental.pallas import tpu as pltpu
from jax.sharding import PartitionSpec as P

MESH = pl.DeviceIdType.MESH
M = 48
T = 144
F = 256
AREAS = 512
LANES = 128
RING = 4
PAD_X = 160
ROWS_Z = 80
PAD_Z = 96
HALF = 64
RAMPS = 132
RAMPS_Z = 68
KEEP_X = 152
KEEP_Z = 88
QUADS = 8
ROWS = 256
capacity_floor = 200.0
spread_floor = 0.05


def iota(shape, dim):
    return lax.broadcasted_iota(jnp.int32, shape, dim)


def swap_halves(u, v):
    low = iota(u.shape, 1) < 4
    first = jnp.where(low, u, pltpu.roll(v, 4, 1))
    second = jnp.where(low, pltpu.roll(u, 4, 1), v)
    return first, second


def ramp_metric(summed, steps, offset, ramps):
    total = jnp.maximum(summed[steps : steps + 1], capacity_floor)
    power = summed[:steps] / total
    wide = jnp.broadcast_to(offset, power.shape).astype(jnp.int32)
    later = power
    for bit in (1, 2, 4, 8):
        later = jnp.where((wide & bit) != 0, pltpu.roll(later, steps - bit, 0), later)
    row = iota(power.shape, 0)
    return jnp.max(jnp.where(row < ramps, later - power, -3e38), axis=0, keepdims=True)


STEP = (0, 0, 1, 1, 3, 3, 2, 2)
BACK = (0, 1, 4, 5, 2, 3, 6, 7)
NEAR = 6
ORDER = (6, 7, 2, 4, 3, 5, 1)


def exchange_kernel(
    tiles, farm_area, capacity, offsets, state, metric_out, slab_out,
    area_in, capacity_in, offsets_in,
    facts_x, facts_z, got_x, got_z, weight_x, weight_z,
    part_x, part_z, sum_x, sum_z, off_x, off_z,
    small, gathered, z_rows, st,
    local_sem, fx_send, fx_recv, fz_send, fz_recv, x_send, x_recv, z_send, z_recv,
    bx_send, bx_recv, bz_send, bz_recv,
    s1_send, s1_recv, s2_send, s2_recv,
):
    g = lax.axis_index("grid")
    y = lax.axis_index("lev")
    z = lax.div(g, 8)
    x = lax.rem(lax.div(g, 2), 4)
    c = lax.rem(g, 2)
    mine_x = 2 * x + c
    mine_z = 2 * z + c
    xs = [x] + [lax.rem(x + d, 4) for d in range(1, 4)]
    zs = [z] + [lax.rem(z + d, 4) for d in range(1, 4)]
    ys = [y] + [lax.rem(y + d, 4) for d in range(1, 4)]
    cs = [c, 1 - c]

    def device(xx, zz, cc, yy):
        return (zz * 8 + xx * 2 + cc, yy)

    sibling = device(x, z, 1 - c, y)
    x_peers = [(xs[STEP[i]], cs[i % 2]) for i in range(8)]
    z_peers = [(zs[STEP[i]], cs[i % 2]) for i in range(8)]

    def remote(src, dst, send_sem, recv_sem, to):
        return pltpu.make_async_remote_copy(
            src_ref=src, dst_ref=dst, send_sem=send_sem, recv_sem=recv_sem,
            device_id=to, device_id_type=MESH)

    def wait_for(slot, send, recv):
        remote(slot, slot, send, recv, sibling).wait_recv()

    def loop(first, last):
        def run(body):
            lax.fori_loop(first, last, lambda i, carry: (body(i), carry)[1], 0)
        return run

    barrier = pltpu.get_barrier_semaphore()

    def greet(to):
        pl.semaphore_signal(barrier, inc=1, device_id=to, device_id_type=MESH)

    for i in ORDER:
        xx, cc = x_peers[i]
        greet(device(xx, z, cc, y))
        if i != 1:
            zz, cc = z_peers[i]
            greet(device(x, zz, cc, y))
    for d in (2, 1, 3):
        greet(device(x, z, c, ys[d]))

    def x_slot(i):
        return got_x.at[pl.ds(0, T), pl.ds(F * i, F)]

    def z_slot(i):
        return got_z.at[pl.ds(0, ROWS_Z), pl.ds(F * i, F)]

    def x_tile(xx, cc):
        return tiles.at[12 * y + 2 * xx + cc]

    def z_tile(zz, cc):
        return tiles.at[12 * y + 8 + zz, pl.ds(pl.multiple_of(HALF * cc, HALF), ROWS_Z)]

    local = [
        pltpu.make_async_copy(farm_area, area_in, local_sem.at[0]),
        pltpu.make_async_copy(capacity, capacity_in, local_sem.at[1]),
        pltpu.make_async_copy(offsets, offsets_in, local_sem.at[2]),
        pltpu.make_async_copy(z_tile(z, c), z_slot(0), local_sem.at[3]),
        pltpu.make_async_copy(x_tile(x, c), x_slot(0), local_sem.at[4]),
        pltpu.make_async_copy(state, st, local_sem.at[5]),
    ]
    for copy in local:
        copy.start()
    for copy in local[:3]:
        copy.wait()

    lane = iota((1, F), 1)
    offset = jnp.zeros((1, F), jnp.int32)
    for k in range(16):
        offset = jnp.where((lane & 15) == k, offsets_in[k], offset)
    area = area_in[...]
    turned = ((area >> 5) & 3) * 128 + (area >> 7) * 32 + (area & 31)
    for facts, ids, spot in ((facts_z, turned, mine_z), (facts_x, area, mine_x)):
        placed = jnp.where((lane >> 4) == spot, offset, 0)
        rows = jnp.concatenate(
            [ids, capacity_in[...], placed, jnp.zeros((1, F), jnp.int32)], axis=0)
        facts[0] = rows.astype(jnp.float32)
    pl.semaphore_wait(barrier, 16)

    def fx_copy(i):
        xx, cc = x_peers[i]
        return remote(facts_x.at[0], facts_x.at[BACK[i]], fx_send.at[i], fx_recv.at[BACK[i]],
                      device(xx, z, cc, y))

    def fz_copy(i):
        zz, cc = z_peers[i]
        return remote(facts_z.at[0], facts_z.at[BACK[i]], fz_send.at[i], fz_recv.at[BACK[i]],
                      device(x, zz, cc, y))

    def x_copy(i):
        xx, cc = x_peers[i]
        return remote(x_tile(xx, cc), x_slot(BACK[i]), x_send.at[i], x_recv.at[BACK[i]],
                      device(xx, z, cc, y))

    def z_copy(i):
        zz, cc = z_peers[i]
        return remote(z_tile(zz, cc), z_slot(BACK[i]), z_send.at[i], z_recv.at[BACK[i]],
                      device(x, zz, cc, y))

    sends = [x_copy(6), x_copy(7), z_copy(6), z_copy(7)]
    sends += [f(i) for i in ORDER for f in (fz_copy, fx_copy)]
    sends += [f(i) for i in ORDER[2:] for f in (x_copy, z_copy)]
    for copy in sends:
        copy.start()

    local[5].wait()

    @loop(0, QUADS)
    def _(i):
        values = st[:, i].astype(jnp.float32).reshape(M, 2, 8, LANES)
        values = values - (jnp.sum(values, axis=0) / M)[None]
        pairs = values.reshape(M // 2, 2, 2, 8, LANES)
        for h in range(2):
            both = swap_halves(pairs[:, 0, h], pairs[:, 1, h])
            for k in range(2):
                slab_out[i, :, pl.ds((2 * h + k) * LANES, LANES)] = (
                    both[k].reshape(4 * M, LANES).astype(jnp.bfloat16))

    got_x[pl.ds(T, 16)] = jnp.ones((16, 8 * F), jnp.bfloat16)
    got_z[pl.ds(ROWS_Z, 16)] = jnp.ones((16, 8 * F), jnp.bfloat16)
    off_x[...] = jnp.zeros_like(off_x)
    off_z[...] = jnp.zeros_like(off_z)
    area_ids = iota((F, AREAS), 1).astype(jnp.float32)

    @loop(0, 8)
    def _(i):
        for facts, recv, send, weight, off in (
                (facts_z, fz_recv, fz_send, weight_z, off_z),
                (facts_x, fx_recv, fx_send, weight_x, off_x)):
            @pl.when(i > 0)
            def _():
                wait_for(facts.at[i], send.at[i], recv.at[i])

            rows = facts[i]
            off[...] = off[...] + rows[2:3, :LANES]
            columns = jnp.transpose(jnp.concatenate([rows, rows], axis=0))
            placed = jnp.where(area_ids == columns[:, 0:1], columns[:, 1:2], 0.0)
            weight[pl.ds(pl.multiple_of(F * i, F), F)] = placed.astype(jnp.bfloat16)

    local[3].wait()
    for i in range(1, 8):
        wait_for(z_slot(i), z_send.at[i], z_recv.at[i])
    for h in range(2):
        value = jnp.dot(got_z[...], weight_z[:, pl.ds(2 * LANES * h, 2 * LANES)],
                        preferred_element_type=jnp.float32)
        for b in range(2):
            part_z[2 * h + b] = value[:KEEP_Z, b * LANES : (b + 1) * LANES]
    bz, bx = [], []
    for d in (2, 1, 3):
        bz.append(remote(part_z.at[xs[d]], sum_z.at[3 - d], bz_send.at[d - 1], bz_recv.at[3 - d],
                         device(xs[d], z, c, y)))
        bz[-1].start()

    local[4].wait()
    for i in range(1, NEAR):
        wait_for(x_slot(i), x_send.at[i], x_recv.at[i])
    near, far = pl.ds(0, NEAR * F), pl.ds(NEAR * F, (8 - NEAR) * F)
    for h in range(2):
        value = jnp.dot(got_x[:, near], weight_x[near, pl.ds(2 * LANES * h, 2 * LANES)],
                        preferred_element_type=jnp.float32)
        for b in range(2):
            part_x[2 * h + b] = value[:KEEP_X, b * LANES : (b + 1) * LANES]
    for i in range(NEAR, 8):
        wait_for(x_slot(i), x_send.at[i], x_recv.at[i])
    for pair in ((2, 1), (3, 0)):
        chosen = jnp.concatenate(
            [weight_x[far, pl.ds(pl.multiple_of(LANES * zs[d], LANES), LANES)] for d in pair],
            axis=1)
        value = jnp.dot(got_x[:, far], chosen, preferred_element_type=jnp.float32)
        for k, d in enumerate(pair):
            part_x[zs[d]] = part_x[zs[d]] + value[:KEEP_X, k * LANES : (k + 1) * LANES]
            if d > 0:
                bx.append(remote(part_x.at[zs[d]], sum_x.at[3 - d], bx_send.at[d - 1],
                                 bx_recv.at[3 - d], device(x, zs[d], c, y)))
                bx[-1].start()

    for copy in bz:
        copy.wait_recv()
    summed = part_z[x] + sum_z[0] + sum_z[1] + sum_z[2]
    small[mine_x, pl.ds(1, 1)] = ramp_metric(summed, ROWS_Z, off_z[...], RAMPS_Z)

    for copy in bx:
        copy.wait_recv()

    summed = part_x[z] + sum_x[0] + sum_x[1] + sum_x[2]
    small[mine_x, pl.ds(0, 1)] = ramp_metric(summed, T, off_x[...], RAMPS)

    def swap(ref, slot, far, send_sem, recv_sem, to):
        copy = remote(ref.at[slot], ref.at[slot], send_sem, recv_sem.at[slot], to)
        copy.start()
        sends.append(copy)
        return remote(ref.at[far], ref.at[far], send_sem, recv_sem.at[far], to)

    back = []
    for i in ORDER:
        xx, cc = x_peers[i]
        back.append(swap(small, mine_x, 2 * xx + cc, s1_send.at[i], s1_recv,
                         device(xx, z, cc, y)))
    for copy in reversed(back):
        copy.wait_recv()

    joined = gathered.at[y, z]
    for s in range(8):
        joined[s // 4, pl.ds(s % 4, 1)] = small[s, pl.ds(0, 1)]
    for b in range(RING):
        joined[2, pl.ds(b, 1)] = jnp.maximum(
            small[2 * b, pl.ds(1, 1)], small[2 * b + 1, pl.ds(1, 1)])

    sends_now = [(dy, dz) for dy in (2, 1, 3, 0) for dz in (2, 1, 3, 0)][:-1]
    back = []
    for k, (dy, dz) in enumerate(sends_now):
        out = remote(joined, joined, s2_send.at[k], s2_recv.at[4 * y + z],
                     device(x, zs[dz], c, ys[dy]))
        out.start()
        sends.append(out)
        slot = gathered.at[ys[dy], zs[dz]]
        back.append((slot, s2_send.at[k], s2_recv.at[4 * ys[dy] + zs[dz]]))
    for slot, send, recv in reversed(back):
        wait_for(slot, send, recv)

    for zz in range(4):
        for yy in range(4):
            slot = 4 * yy + zz
            for h in range(2):
                metric_out[pl.ds(8 * yy + 4 * h, 4), pl.ds(zz * LANES, LANES)] = gathered[yy, zz, h]
            for b in range(RING):
                z_rows[b, pl.ds(slot, 1)] = gathered[yy, zz, 2, pl.ds(b, 1)]
    quarter = iota((16, LANES), 1) >> 5
    blocks = [z_rows[b] for b in range(RING)]
    for zz in range(4):
        value = jnp.zeros((16, LANES), jnp.float32)
        for b in range(RING):
            move = (32 * (b - zz)) % LANES
            moved = pltpu.roll(blocks[b], move, 1) if move else blocks[b]
            value = jnp.where(quarter == b, moved, value)
        metric_out[pl.ds(32, 16), pl.ds(zz * LANES, LANES)] = value

    for copy in sends + bx + bz:
        copy.wait_send()


def exchange(tiles, farm_area, capacity, offsets, state):
    any_space = pl.BlockSpec(memory_space=pl.ANY)
    vmem = pl.BlockSpec(memory_space=pltpu.VMEM)
    dma = pltpu.SemaphoreType.DMA
    f32, bf16 = jnp.float32, jnp.bfloat16
    return pl.pallas_call(
        exchange_kernel,
        out_shape=(
            pltpu.VMEM((M, AREAS), f32),
            pltpu.VMEM((QUADS, 4 * M, 4 * LANES), bf16),
        ),
        in_specs=[any_space] * 5,
        out_specs=(vmem, vmem),
        scratch_shapes=[
            pltpu.VMEM((1, F), jnp.int32),
            pltpu.VMEM((1, F), jnp.int32),
            pltpu.SMEM((16,), jnp.int32),
            pltpu.VMEM((8, 4, F), f32),
            pltpu.VMEM((8, 4, F), f32),
            pltpu.VMEM((PAD_X, 8 * F), bf16),
            pltpu.VMEM((PAD_Z, 8 * F), bf16),
            pltpu.VMEM((8 * F, AREAS), bf16),
            pltpu.VMEM((8 * F, AREAS), bf16),
            pltpu.VMEM((RING, KEEP_X, LANES), f32),
            pltpu.VMEM((RING, KEEP_Z, LANES), f32),
            pltpu.VMEM((3, KEEP_X, LANES), f32),
            pltpu.VMEM((3, KEEP_Z, LANES), f32),
            pltpu.VMEM((1, LANES), f32),
            pltpu.VMEM((1, LANES), f32),
            pltpu.VMEM((8, 2, LANES), f32),
            pltpu.VMEM((4, 4, 3, 4, LANES), f32),
            pltpu.VMEM((RING, 16, LANES), f32),
            pltpu.VMEM((M, QUADS, 16, LANES), bf16),
            dma((6,)), dma((8,)), dma((8,)), dma((8,)), dma((8,)),
            dma((8,)), dma((8,)), dma((8,)), dma((8,)),
            dma((3,)), dma((3,)), dma((3,)), dma((3,)),
            dma((8,)), dma((8,)), dma((16,)), dma((16,)),
        ],
        compiler_params=pltpu.CompilerParams(
            collective_id=0, has_side_effects=True, vmem_limit_bytes=60 * 2**20),
        cost_estimate=pl.CostEstimate(
            flops=2 * 256 * 2048 * 512, bytes_accessed=5 * 2**20, transcendentals=0),
        name="exchange",
    )(tiles, farm_area, capacity, offsets, state)


def product_kernel(metric, slab, out, wide, lhs, stage, out_sem):
    values = metric[...]
    anomaly = values - jnp.mean(values, axis=0, keepdims=True)
    spread = jnp.sqrt(jnp.sum(anomaly * anomaly, axis=0, keepdims=True) / (M - 1))
    scores = anomaly / jnp.maximum(spread, spread_floor)
    scores = jnp.transpose(scores).astype(jnp.bfloat16)

    held = iota((M, 4 * M), 0)
    rest = held - 32
    member = jnp.where(
        held < 32,
        12 * (held >> 3) + (held & 7),
        12 * (rest >> 2) + 8 + (rest & 3))
    widen = ((iota((M, 4 * M), 1) >> 2) == member).astype(jnp.bfloat16)
    wide[...] = jnp.dot(scores, widen, preferred_element_type=jnp.float32).astype(jnp.bfloat16)
    repeat = ((iota((ROWS, ROWS // 4), 0) >> 2) == iota((ROWS, ROWS // 4), 1)).astype(
        jnp.bfloat16)
    keep = (iota((ROWS, 4 * M), 0) & 3) == (iota((ROWS, 4 * M), 1) & 3)
    areas = ROWS // 4

    for r in range(4 * AREAS // ROWS):
        rows = jnp.dot(repeat, wide[pl.ds(r * areas, areas)], preferred_element_type=jnp.float32)
        lhs[pl.ds(r * ROWS, ROWS)] = jnp.where(keep, rows, 0.0).astype(jnp.bfloat16)

    def part(i, q):
        some = pl.ds(128 * q, 128)
        return pltpu.make_async_copy(stage.at[i, some], out.at[some, i], out_sem.at[4 * i + q])

    def step(j, carry):
        for k in range(2):
            i = 2 * j + k
            for r in range(4 * AREAS // ROWS):
                left = lhs[pl.ds(r * ROWS, ROWS)]
                parts = []
                for h in range(2):
                    acc = jnp.dot(left, slab[i, :, pl.ds(2 * LANES * h, 2 * LANES)],
                                  preferred_element_type=jnp.float32)
                    acc = (acc * (1.0 / (M - 1))).reshape(ROWS // 8, 8, 2 * LANES)
                    both = swap_halves(acc[:, :, :LANES], acc[:, :, LANES:])
                    parts.append(jnp.stack(both, axis=1).reshape(areas, 8, LANES))
                done = jnp.stack(parts, axis=1).reshape(areas, 16, LANES)
                stage[i, pl.ds(r * areas, areas)] = done.astype(jnp.bfloat16)
                if (r + 1) * areas % 128 == 0:
                    part(i, r * areas // 128).start()
        return carry

    lax.fori_loop(0, QUADS // 2, step, 0)

    def finish(i, carry):
        for q in range(4):
            part(i, q).wait()
        return carry

    lax.fori_loop(0, QUADS, finish, 0)


def product(metric, slab):
    any_space = pl.BlockSpec(memory_space=pl.ANY)
    dma = pltpu.SemaphoreType.DMA
    return pl.pallas_call(
        product_kernel,
        out_shape=jax.ShapeDtypeStruct((AREAS, QUADS, 16, LANES), jnp.bfloat16),
        in_specs=[pl.BlockSpec(memory_space=pltpu.VMEM)] * 2,
        out_specs=any_space,
        scratch_shapes=[
            pltpu.VMEM((AREAS, 4 * M), jnp.bfloat16),
            pltpu.VMEM((4 * AREAS, 4 * M), jnp.bfloat16),
            pltpu.VMEM((QUADS, AREAS, 16, LANES), jnp.bfloat16),
            dma((32,)),
        ],
        compiler_params=pltpu.CompilerParams(vmem_limit_bytes=32 * 2**20),
        cost_estimate=pl.CostEstimate(
            flops=2 * 2048 * 192 * 4096, bytes_accessed=20 * 2**20, transcendentals=0),
        name="product",
    )(metric, slab)


def body(tiles, farm_area, capacity, offsets, state):
    by_member = jnp.transpose(tiles, (1, 2, 0))
    columns = state.reshape(M, 2, 64, LANES)
    columns = jnp.transpose(columns, (0, 2, 1, 3)).reshape(M, QUADS, 16, LANES)
    metric, slab = exchange(
        by_member, farm_area.reshape(1, F), capacity.reshape(1, F), offsets, columns)
    out = product(metric, slab)
    out = jnp.transpose(out.reshape(AREAS, 64, 2, LANES), (0, 2, 1, 3))
    return out.reshape(AREAS, 2, 64 * LANES)


def solution(mesh):
    in_specs = (P("grid", None, None), P("grid"), P("grid"), P("grid"), P(None, "lev", "grid"))
    out_specs = P(None, "lev", "grid")
    return jax.shard_map(body, mesh=mesh, in_specs=in_specs, out_specs=out_specs, check_vma=False)
```

time: 191 us -> 40.1 us (0.21)
  waiting for transfers between devices: 73.6 us -> 0 us
  Pallas kernels: 0 us -> 40 us
  local copies, waits for them, and re-layouts: 35.6 us -> 0 us
  blocking collectives: 28.4 us -> 0 us
  matrix products: 25.9 us -> 0 us
  starting transfers between devices: 15.6 us -> 0 us
  other arithmetic: 10 us -> 0 us
    all_to_all x2 -> x0, waiting for transfers between devices: 73.6 us -> none  [the longest x1 72.3 us: body(): lax.all_to_all(outgoing.reshape(owners, slots, members * steps), 'grid',...]
    pallas_call x0 -> x2, Pallas kernels: none -> 40 us  [the longest x1 32.9 us: exchange(): pl.pallas_call(exchange_kernel, out_shape=(pltpu.VMEM((M, AREAS), f32), p...]
    reshape x5 -> x0, local copies, waits for them, and re-layouts: 32.4 us -> none  [the longest x1 27.7 us: body(): return result.reshape(result.shape[0], state.shape[1], state.shape[2])]
    all_gather x1 -> x0, blocking collectives: 28.4 us -> none  [body(): lax.all_gather(scores, 'grid', axis=1, tiled=True)]
    dot_general x5 -> x0, matrix products: 25.9 us -> none  [the longest x1 11.7 us: body(): lax.dot_general(lax.all_gather(scores, 'grid', axis=1, tiled=True), slab,...]
    all_to_all x2 -> x0, starting transfers between devices: 15.6 us -> none  [the longest x1 9.43 us: body(): lax.all_to_all(out_labels.reshape(owners, slots, 2), 'grid', split_axis=0...]
    reduce_sum x5 -> x0, other arithmetic: 3.92 us -> none  [the longest x1 2.69 us: body(): slab = (wide - jnp.mean(wide, axis=0, keepdims=True)).astype(jnp.bfloat16)]
    convert_element_type x2 -> x0, other arithmetic: 3.14 us -> none  [the longest x1 3.06 us: body(): slab = (wide - jnp.mean(wide, axis=0, keepdims=True)).astype(jnp.bfloat16)]
  transfers between devices with their start and end apart: 2 -> 0, of which waited for: 2 -> 0; matrix products, arithmetic and copies ran while one was open for 9% -> 0% of each run, Pallas kernels for 0% -> 0%
where the time goes in v1:
time: 40.1 us; the launch traced here: 40 us
  Pallas kernels  40 us (100%)
    pallas_call x1, Pallas kernels, exchange(): pl.pallas_call(exchange_kernel, out_shape=(pltpu.VMEM((M, AREAS), f32), p...  32.9 us
    pallas_call x1, Pallas kernels, product(): pl.pallas_call(product_kernel, out_shape=jax.ShapeDtypeStruct((AREAS, QUA...  7.11 us

profile of v1, /device:TPU:1, one launch (start us, length us, event | category | flops | bytes accessed | tf_op | source)
XLA Modules:
  0.0 40.0 jit_solution(2941302161273163491)
XLA Ops:
  0.0 32.9 %exchange.1 = (f32[48,512]{1,0:T(8,128)S(1)}, bf16[8,192,512]{2,1,0:T(8,128)(2,1)S(1)}) custom-call(bf16[48,144,256]{2,1,0:T(8,128)(2,1)} %bitcast.13, s32[1,256]{1,0:T(1,128)} %bitcast.15, s32[1,256]{1,0:T(1,128)} %bitcast.16, s32[16]{0:T(128)} %offsets.1, bf16[48,8,16,128]{3,2,1,0:T(8,128)(2,1)} %bitcast.14), custom_call_target="tpu_custom_call" | custom-call | flops 536870912 | bytes 5242880 | tf_op jit(solution)/shard_map/exchange/pallas_call | solution.py:318
  32.9 7.1 %product.1 = bf16[512,8,16,128]{3,2,1,0:T(8,128)(2,1)} custom-call(f32[48,512]{1,0:T(8,128)S(1)} %get-tuple-element.7.metric, bf16[8,192,512]{2,1,0:T(8,128)(2,1)S(1)} %get-tuple-element.8.slab), custom_call_target="tpu_custom_call" | custom-call | flops 3221225472 | bytes 20971520 | tf_op jit(solution)/shard_map/product/pallas_call | solution.py:418

commit v2 on v1

--- a/solution.py
+++ b/solution.py
@@ -50,8 +50,9 @@
 
 STEP = (0, 0, 1, 1, 3, 3, 2, 2)
 BACK = (0, 1, 4, 5, 2, 3, 6, 7)
-NEAR = 6
 ORDER = (6, 7, 2, 4, 3, 5, 1)
+FIRST = 80
+HALVES = (pl.ds(0, FIRST), pl.ds(FIRST, T - FIRST))
 
 
 def exchange_kernel(
@@ -110,8 +111,8 @@
     for d in (2, 1, 3):
         greet(device(x, z, c, ys[d]))
 
-    def x_slot(i):
-        return got_x.at[pl.ds(0, T), pl.ds(F * i, F)]
+    def x_slot(i, half):
+        return got_x.at[HALVES[half], pl.ds(F * i, F)]
 
     def z_slot(i):
         return got_z.at[pl.ds(0, ROWS_Z), pl.ds(F * i, F)]
@@ -127,11 +128,41 @@
         pltpu.make_async_copy(capacity, capacity_in, local_sem.at[1]),
         pltpu.make_async_copy(offsets, offsets_in, local_sem.at[2]),
         pltpu.make_async_copy(z_tile(z, c), z_slot(0), local_sem.at[3]),
-        pltpu.make_async_copy(x_tile(x, c), x_slot(0), local_sem.at[4]),
+        pltpu.make_async_copy(x_tile(x, c), got_x.at[pl.ds(0, T), pl.ds(0, F)], local_sem.at[4]),
         pltpu.make_async_copy(state, st, local_sem.at[5]),
     ]
     for copy in local:
         copy.start()
+    pl.semaphore_wait(barrier, 16)
+
+    def fx_copy(i):
+        xx, cc = x_peers[i]
+        return remote(facts_x.at[0], facts_x.at[BACK[i]], fx_send.at[i], fx_recv.at[BACK[i]],
+                      device(xx, z, cc, y))
+
+    def fz_copy(i):
+        zz, cc = z_peers[i]
+        return remote(facts_z.at[0], facts_z.at[BACK[i]], fz_send.at[i], fz_recv.at[BACK[i]],
+                      device(x, zz, cc, y))
+
+    def x_copy(i, half):
+        xx, cc = x_peers[i]
+        return remote(x_tile(xx, cc).at[HALVES[half]], x_slot(BACK[i], half),
+                      x_send.at[half, i], x_recv.at[half, BACK[i]], device(xx, z, cc, y))
+
+    def z_copy(i):
+        zz, cc = z_peers[i]
+        return remote(z_tile(zz, cc), z_slot(BACK[i]), z_send.at[i], z_recv.at[BACK[i]],
+                      device(x, zz, cc, y))
+
+    sends = []
+
+    def start(*copies):
+        for copy in copies:
+            copy.start()
+            sends.append(copy)
+
+    start(x_copy(6, 0), x_copy(7, 0), z_copy(6), z_copy(7))
     for copy in local[:3]:
         copy.wait()
 
@@ -146,33 +177,11 @@
         rows = jnp.concatenate(
             [ids, capacity_in[...], placed, jnp.zeros((1, F), jnp.int32)], axis=0)
         facts[0] = rows.astype(jnp.float32)
-    pl.semaphore_wait(barrier, 16)
-
-    def fx_copy(i):
-        xx, cc = x_peers[i]
-        return remote(facts_x.at[0], facts_x.at[BACK[i]], fx_send.at[i], fx_recv.at[BACK[i]],
-                      device(xx, z, cc, y))
-
-    def fz_copy(i):
-        zz, cc = z_peers[i]
-        return remote(facts_z.at[0], facts_z.at[BACK[i]], fz_send.at[i], fz_recv.at[BACK[i]],
-                      device(x, zz, cc, y))
-
-    def x_copy(i):
-        xx, cc = x_peers[i]
-        return remote(x_tile(xx, cc), x_slot(BACK[i]), x_send.at[i], x_recv.at[BACK[i]],
-                      device(xx, z, cc, y))
-
-    def z_copy(i):
-        zz, cc = z_peers[i]
-        return remote(z_tile(zz, cc), z_slot(BACK[i]), z_send.at[i], z_recv.at[BACK[i]],
-                      device(x, zz, cc, y))
-
-    sends = [x_copy(6), x_copy(7), z_copy(6), z_copy(7)]
-    sends += [f(i) for i in ORDER for f in (fz_copy, fx_copy)]
-    sends += [f(i) for i in ORDER[2:] for f in (x_copy, z_copy)]
-    for copy in sends:
-        copy.start()
+
+    for i in ORDER:
+        start(fz_copy(i), fx_copy(i))
+    for i in ORDER[2:]:
+        start(x_copy(i, 0), z_copy(i))
 
     local[5].wait()
 
@@ -187,6 +196,9 @@
                 slab_out[i, :, pl.ds((2 * h + k) * LANES, LANES)] = (
                     both[k].reshape(4 * M, LANES).astype(jnp.bfloat16))
 
+    for i in ORDER:
+        start(x_copy(i, 1))
+
     got_x[pl.ds(T, 16)] = jnp.ones((16, 8 * F), jnp.bfloat16)
     got_z[pl.ds(ROWS_Z, 16)] = jnp.ones((16, 8 * F), jnp.bfloat16)
     off_x[...] = jnp.zeros_like(off_x)
@@ -216,34 +228,33 @@
                         preferred_element_type=jnp.float32)
         for b in range(2):
             part_z[2 * h + b] = value[:KEEP_Z, b * LANES : (b + 1) * LANES]
+    local[4].wait()
     bz, bx = [], []
+
+    def part_copy(d, half, first, count):
+        rows = pl.ds(first, count)
+        return remote(part_x.at[zs[d], rows], sum_x.at[3 - d, rows], bx_send.at[half, d - 1],
+                      bx_recv.at[half, 3 - d], device(x, zs[d], c, y))
+
+    for half, (first, count, keep) in enumerate(
+            ((0, FIRST, FIRST), (FIRST, PAD_X - FIRST, KEEP_X - FIRST))):
+        for i in range(1, 8):
+            wait_for(x_slot(i, half), x_send.at[half, i], x_recv.at[half, i])
+        for pair in ((2, 1), (3, 0)):
+            chosen = jnp.concatenate(
+                [weight_x[:, pl.ds(pl.multiple_of(LANES * zs[d], LANES), LANES)] for d in pair],
+                axis=1)
+            value = jnp.dot(got_x[pl.ds(first, count)], chosen,
+                            preferred_element_type=jnp.float32)
+            for k, d in enumerate(pair):
+                part_x[zs[d], pl.ds(first, keep)] = value[:keep, k * LANES : (k + 1) * LANES]
+                if d > 0:
+                    bx.append(part_copy(d, half, first, keep))
+                    bx[-1].start()
     for d in (2, 1, 3):
         bz.append(remote(part_z.at[xs[d]], sum_z.at[3 - d], bz_send.at[d - 1], bz_recv.at[3 - d],
                          device(xs[d], z, c, y)))
         bz[-1].start()
-
-    local[4].wait()
-    for i in range(1, NEAR):
-        wait_for(x_slot(i), x_send.at[i], x_recv.at[i])
-    near, far = pl.ds(0, NEAR * F), pl.ds(NEAR * F, (8 - NEAR) * F)
-    for h in range(2):
-        value = jnp.dot(got_x[:, near], weight_x[near, pl.ds(2 * LANES * h, 2 * LANES)],
-                        preferred_element_type=jnp.float32)
-        for b in range(2):
-            part_x[2 * h + b] = value[:KEEP_X, b * LANES : (b + 1) * LANES]
-    for i in range(NEAR, 8):
-        wait_for(x_slot(i), x_send.at[i], x_recv.at[i])
-    for pair in ((2, 1), (3, 0)):
-        chosen = jnp.concatenate(
-            [weight_x[far, pl.ds(pl.multiple_of(LANES * zs[d], LANES), LANES)] for d in pair],
-            axis=1)
-        value = jnp.dot(got_x[:, far], chosen, preferred_element_type=jnp.float32)
-        for k, d in enumerate(pair):
-            part_x[zs[d]] = part_x[zs[d]] + value[:KEEP_X, k * LANES : (k + 1) * LANES]
-            if d > 0:
-                bx.append(remote(part_x.at[zs[d]], sum_x.at[3 - d], bx_send.at[d - 1],
-                                 bx_recv.at[3 - d], device(x, zs[d], c, y)))
-                bx[-1].start()
 
     for copy in bz:
         copy.wait_recv()
@@ -344,8 +355,8 @@
             pltpu.VMEM((RING, 16, LANES), f32),
             pltpu.VMEM((M, QUADS, 16, LANES), bf16),
             dma((6,)), dma((8,)), dma((8,)), dma((8,)), dma((8,)),
-            dma((8,)), dma((8,)), dma((8,)), dma((8,)),
-            dma((3,)), dma((3,)), dma((3,)), dma((3,)),
+            dma((2, 8)), dma((2, 8)), dma((8,)), dma((8,)),
+            dma((2, 3)), dma((2, 3)), dma((3,)), dma((3,)),
             dma((8,)), dma((8,)), dma((16,)), dma((16,)),
         ],
         compiler_params=pltpu.CompilerParams(

time: 40.1 us -> 38.8 us (0.968)
  Pallas kernels: 40 us -> 38.7 us
    pallas_call x1, Pallas kernels: 32.9 us -> 31.6 us  [exchange(): pl.pallas_call(exchange_kernel, out_shape=(pltpu.VMEM((M, AREAS), f32), p...]
where the time goes in v2:
time: 38.8 us; the launch traced here: 38.7 us
  Pallas kernels  38.7 us (100%)
    pallas_call x1, Pallas kernels, exchange(): pl.pallas_call(exchange_kernel, out_shape=(pltpu.VMEM((M, AREAS), f32), p...  31.6 us
    pallas_call x1, Pallas kernels, product(): pl.pallas_call(product_kernel, out_shape=jax.ShapeDtypeStruct((AREAS, QUA...  7.1 us

profile of v2, /device:TPU:1, one launch (start us, length us, event | category | flops | bytes accessed | tf_op | source)
XLA Modules:
  0.0 38.7 jit_solution(3976580161879602155)
XLA Ops:
  0.0 31.6 %exchange.1 = (f32[48,512]{1,0:T(8,128)S(1)}, bf16[8,192,512]{2,1,0:T(8,128)(2,1)S(1)}) custom-call(bf16[48,144,256]{2,1,0:T(8,128)(2,1)} %bitcast.13, s32[1,256]{1,0:T(1,128)} %bitcast.15, s32[1,256]{1,0:T(1,128)} %bitcast.16, s32[16]{0:T(128)} %offsets.1, bf16[48,8,16,128]{3,2,1,0:T(8,128)(2,1)} %bitcast.14), custom_call_target="tpu_custom_call" | custom-call | flops 536870912 | bytes 5242880 | tf_op jit(solution)/shard_map/exchange/pallas_call | solution.py:329
  31.6 7.1 %product.1 = bf16[512,8,16,128]{3,2,1,0:T(8,128)(2,1)} custom-call(f32[48,512]{1,0:T(8,128)S(1)} %get-tuple-element.7.metric, bf16[8,192,512]{2,1,0:T(8,128)(2,1)S(1)} %get-tuple-element.8.slab), custom_call_target="tpu_custom_call" | custom-call | flops 3221225472 | bytes 20971520 | tf_op jit(solution)/shard_map/product/pallas_call | solution.py:429

commit v3 on v2

--- a/solution.py
+++ b/solution.py
@@ -183,6 +183,70 @@
     for i in ORDER[2:]:
         start(x_copy(i, 0), z_copy(i))
 
+    for i in ORDER:
+        start(x_copy(i, 1))
+
+    got_x[pl.ds(T, 16)] = jnp.ones((16, 8 * F), jnp.bfloat16)
+    got_z[pl.ds(ROWS_Z, 16)] = jnp.ones((16, 8 * F), jnp.bfloat16)
+    off_x[...] = jnp.zeros_like(off_x)
+    off_z[...] = jnp.zeros_like(off_z)
+    area_ids = iota((AREAS, F), 0).astype(jnp.float32)
+
+    def weigh(i, facts, weight, off):
+        rows = facts[i]
+        off[...] = off[...] + rows[2:3, :LANES]
+        placed = jnp.where(area_ids == rows[0:1], rows[1:2], 0.0)
+        weight[:, pl.ds(pl.multiple_of(F * i, F), F)] = placed.astype(jnp.bfloat16)
+
+    @loop(0, 8)
+    def _(i):
+        for facts, recv, send, weight, off in (
+                (facts_z, fz_recv, fz_send, weight_z, off_z),
+                (facts_x, fx_recv, fx_send, weight_x, off_x)):
+            @pl.when(i > 0)
+            def _():
+                wait_for(facts.at[i], send.at[i], recv.at[i])
+
+            weigh(i, facts, weight, off)
+
+    def sum_up(values, weights):
+        return lax.dot_general(values, weights, (((1,), (1,)), ((), ())),
+                               preferred_element_type=jnp.float32)
+
+    local[3].wait()
+    for i in range(1, 8):
+        wait_for(z_slot(i), z_send.at[i], z_recv.at[i])
+    for h in range(2):
+        value = sum_up(got_z[...], weight_z[pl.ds(2 * LANES * h, 2 * LANES)])
+        for b in range(2):
+            part_z[2 * h + b] = value[:KEEP_Z, b * LANES : (b + 1) * LANES]
+    local[4].wait()
+    bz, bx = [], []
+
+    def part_copy(d, half, first, count):
+        rows = pl.ds(first, count)
+        return remote(part_x.at[zs[d], rows], sum_x.at[3 - d, rows], bx_send.at[half, d - 1],
+                      bx_recv.at[half, 3 - d], device(x, zs[d], c, y))
+
+    for half, (first, count, keep) in enumerate(
+            ((0, FIRST, FIRST), (FIRST, PAD_X - FIRST, KEEP_X - FIRST))):
+        for i in range(1, 8):
+            wait_for(x_slot(i, half), x_send.at[half, i], x_recv.at[half, i])
+        for pair in ((2, 1), (3, 0)):
+            chosen = jnp.concatenate(
+                [weight_x[pl.ds(pl.multiple_of(LANES * zs[d], LANES), LANES)] for d in pair],
+                axis=0)
+            value = sum_up(got_x[pl.ds(first, count)], chosen)
+            for k, d in enumerate(pair):
+                part_x[zs[d], pl.ds(first, keep)] = value[:keep, k * LANES : (k + 1) * LANES]
+                if d > 0:
+                    bx.append(part_copy(d, half, first, keep))
+                    bx[-1].start()
+    for d in (2, 1, 3):
+        bz.append(remote(part_z.at[xs[d]], sum_z.at[3 - d], bz_send.at[d - 1], bz_recv.at[3 - d],
+                         device(xs[d], z, c, y)))
+        bz[-1].start()
+
     local[5].wait()
 
     @loop(0, QUADS)
@@ -195,66 +259,6 @@
             for k in range(2):
                 slab_out[i, :, pl.ds((2 * h + k) * LANES, LANES)] = (
                     both[k].reshape(4 * M, LANES).astype(jnp.bfloat16))
-
-    for i in ORDER:
-        start(x_copy(i, 1))
-
-    got_x[pl.ds(T, 16)] = jnp.ones((16, 8 * F), jnp.bfloat16)
-    got_z[pl.ds(ROWS_Z, 16)] = jnp.ones((16, 8 * F), jnp.bfloat16)
-    off_x[...] = jnp.zeros_like(off_x)
-    off_z[...] = jnp.zeros_like(off_z)
-    area_ids = iota((F, AREAS), 1).astype(jnp.float32)
-
-    @loop(0, 8)
-    def _(i):
-        for facts, recv, send, weight, off in (
-                (facts_z, fz_recv, fz_send, weight_z, off_z),
-                (facts_x, fx_recv, fx_send, weight_x, off_x)):
-            @pl.when(i > 0)
-            def _():
-                wait_for(facts.at[i], send.at[i], recv.at[i])
-
-            rows = facts[i]
-            off[...] = off[...] + rows[2:3, :LANES]
-            columns = jnp.transpose(jnp.concatenate([rows, rows], axis=0))
-            placed = jnp.where(area_ids == columns[:, 0:1], columns[:, 1:2], 0.0)
-            weight[pl.ds(pl.multiple_of(F * i, F), F)] = placed.astype(jnp.bfloat16)
-
-    local[3].wait()
-    for i in range(1, 8):
-        wait_for(z_slot(i), z_send.at[i], z_recv.at[i])
-    for h in range(2):
-        value = jnp.dot(got_z[...], weight_z[:, pl.ds(2 * LANES * h, 2 * LANES)],
-                        preferred_element_type=jnp.float32)
-        for b in range(2):
-            part_z[2 * h + b] = value[:KEEP_Z, b * LANES : (b + 1) * LANES]
-    local[4].wait()
-    bz, bx = [], []
-
-    def part_copy(d, half, first, count):
-        rows = pl.ds(first, count)
-        return remote(part_x.at[zs[d], rows], sum_x.at[3 - d, rows], bx_send.at[half, d - 1],
-                      bx_recv.at[half, 3 - d], device(x, zs[d], c, y))
-
-    for half, (first, count, keep) in enumerate(
-            ((0, FIRST, FIRST), (FIRST, PAD_X - FIRST, KEEP_X - FIRST))):
-        for i in range(1, 8):
-            wait_for(x_slot(i, half), x_send.at[half, i], x_recv.at[half, i])
-        for pair in ((2, 1), (3, 0)):
-            chosen = jnp.concatenate(
-                [weight_x[:, pl.ds(pl.multiple_of(LANES * zs[d], LANES), LANES)] for d in pair],
-                axis=1)
-            value = jnp.dot(got_x[pl.ds(first, count)], chosen,
-                            preferred_element_type=jnp.float32)
-            for k, d in enumerate(pair):
-                part_x[zs[d], pl.ds(first, keep)] = value[:keep, k * LANES : (k + 1) * LANES]
-                if d > 0:
-                    bx.append(part_copy(d, half, first, keep))
-                    bx[-1].start()
-    for d in (2, 1, 3):
-        bz.append(remote(part_z.at[xs[d]], sum_z.at[3 - d], bz_send.at[d - 1], bz_recv.at[3 - d],
-                         device(xs[d], z, c, y)))
-        bz[-1].start()
 
     for copy in bz:
         copy.wait_recv()
@@ -342,8 +346,8 @@
             pltpu.VMEM((8, 4, F), f32),
             pltpu.VMEM((PAD_X, 8 * F), bf16),
             pltpu.VMEM((PAD_Z, 8 * F), bf16),
-            pltpu.VMEM((8 * F, AREAS), bf16),
-            pltpu.VMEM((8 * F, AREAS), bf16),
+            pltpu.VMEM((AREAS, 8 * F), bf16),
+            pltpu.VMEM((AREAS, 8 * F), bf16),
             pltpu.VMEM((RING, KEEP_X, LANES), f32),
             pltpu.VMEM((RING, KEEP_Z, LANES), f32),
             pltpu.VMEM((3, KEEP_X, LANES), f32),
@@ -387,19 +391,21 @@
     keep = (iota((ROWS, 4 * M), 0) & 3) == (iota((ROWS, 4 * M), 1) & 3)
     areas = ROWS // 4
 
-    for r in range(4 * AREAS // ROWS):
+    def make(r):
         rows = jnp.dot(repeat, wide[pl.ds(r * areas, areas)], preferred_element_type=jnp.float32)
-        lhs[pl.ds(r * ROWS, ROWS)] = jnp.where(keep, rows, 0.0).astype(jnp.bfloat16)
+        left = jnp.where(keep, rows, 0.0).astype(jnp.bfloat16)
+        lhs[pl.ds(r * ROWS, ROWS)] = left
+        return left
 
     def part(i, q):
         some = pl.ds(128 * q, 128)
         return pltpu.make_async_copy(stage.at[i, some], out.at[some, i], out_sem.at[4 * i + q])
 
-    def step(j, carry):
+    def step(j, carry, fresh=False):
         for k in range(2):
             i = 2 * j + k
             for r in range(4 * AREAS // ROWS):
-                left = lhs[pl.ds(r * ROWS, ROWS)]
+                left = make(r) if fresh and k == 0 else lhs[pl.ds(r * ROWS, ROWS)]
                 parts = []
                 for h in range(2):
                     acc = jnp.dot(left, slab[i, :, pl.ds(2 * LANES * h, 2 * LANES)],
@@ -413,7 +419,8 @@
                     part(i, r * areas // 128).start()
         return carry
 
-    lax.fori_loop(0, QUADS // 2, step, 0)
+    step(0, 0, fresh=True)
+    lax.fori_loop(1, QUADS // 2, step, 0)
 
     def finish(i, carry):
         for q in range(4):

time: 38.8 us -> 39.9 us (1.028)
  Pallas kernels: 38.7 us -> 39.8 us
    pallas_call x1, Pallas kernels: 7.1 us -> 8.03 us  [product(): pl.pallas_call(product_kernel, out_shape=jax.ShapeDtypeStruct((AREAS, QUA...]
where the time goes in v3:
time: 39.9 us
  Pallas kernels  39.8 us (100%)
    pallas_call x1, Pallas kernels, exchange(): pl.pallas_call(exchange_kernel, out_shape=(pltpu.VMEM((M, AREAS), f32), p...  31.8 us
    pallas_call x1, Pallas kernels, product(): pl.pallas_call(product_kernel, out_shape=jax.ShapeDtypeStruct((AREAS, QUA...  8.03 us

profile of v3, /device:TPU:1, one launch (start us, length us, event | category | flops | bytes accessed | tf_op | source)
XLA Modules:
  0.0 39.9 jit_solution(4884321928466437912)
XLA Ops:
  0.0 31.8 %exchange.1 = (f32[48,512]{1,0:T(8,128)S(1)}, bf16[8,192,512]{2,1,0:T(8,128)(2,1)S(1)}) custom-call(bf16[48,144,256]{2,1,0:T(8,128)(2,1)} %bitcast.13, s32[1,256]{1,0:T(1,128)} %bitcast.15, s32[1,256]{1,0:T(1,128)} %bitcast.16, s32[16]{0:T(128)} %offsets.1, bf16[48,8,16,128]{3,2,1,0:T(8,128)(2,1)} %bitcast.14), custom_call_target="tpu_custom_call" | custom-call | flops 536870912 | bytes 5242880 | tf_op jit(solution)/shard_map/exchange/pallas_call | solution.py:333
  31.8 8.0 %product.1 = bf16[512,8,16,128]{3,2,1,0:T(8,128)(2,1)} custom-call(f32[48,512]{1,0:T(8,128)S(1)} %get-tuple-element.7.metric, bf16[8,192,512]{2,1,0:T(8,128)(2,1)S(1)} %get-tuple-element.8.slab), custom_call_target="tpu_custom_call" | custom-call | flops 3221225472 | bytes 20971520 | tf_op jit(solution)/shard_map/product/pallas_call | solution.py:436

commit v4 on v3

--- a/solution.py
+++ b/solution.py
@@ -32,9 +32,8 @@
 
 def swap_halves(u, v):
     low = iota(u.shape, 1) < 4
-    first = jnp.where(low, u, pltpu.roll(v, 4, 1))
-    second = jnp.where(low, pltpu.roll(u, 4, 1), v)
-    return first, second
+    crossed = pltpu.roll(jnp.where(low, v, u), 4, 1)
+    return jnp.where(low, u, crossed), jnp.where(low, crossed, v)
 
 
 def ramp_metric(summed, steps, offset, ramps):
@@ -51,7 +50,7 @@
 STEP = (0, 0, 1, 1, 3, 3, 2, 2)
 BACK = (0, 1, 4, 5, 2, 3, 6, 7)
 ORDER = (6, 7, 2, 4, 3, 5, 1)
-FIRST = 80
+FIRST = 96
 HALVES = (pl.ds(0, FIRST), pl.ds(FIRST, T - FIRST))
 
 
@@ -232,6 +231,11 @@
             ((0, FIRST, FIRST), (FIRST, PAD_X - FIRST, KEEP_X - FIRST))):
         for i in range(1, 8):
             wait_for(x_slot(i, half), x_send.at[half, i], x_recv.at[half, i])
+        if half == 1:
+            for d in (2, 1, 3):
+                bz.append(remote(part_z.at[xs[d]], sum_z.at[3 - d], bz_send.at[d - 1], bz_recv.at[3 - d],
+                                 device(xs[d], z, c, y)))
+                bz[-1].start()
         for pair in ((2, 1), (3, 0)):
             chosen = jnp.concatenate(
                 [weight_x[pl.ds(pl.multiple_of(LANES * zs[d], LANES), LANES)] for d in pair],
@@ -242,11 +246,6 @@
                 if d > 0:
                     bx.append(part_copy(d, half, first, keep))
                     bx[-1].start()
-    for d in (2, 1, 3):
-        bz.append(remote(part_z.at[xs[d]], sum_z.at[3 - d], bz_send.at[d - 1], bz_recv.at[3 - d],
-                         device(xs[d], z, c, y)))
-        bz[-1].start()
-
     local[5].wait()
 
     @loop(0, QUADS)
@@ -292,6 +291,8 @@
         joined[2, pl.ds(b, 1)] = jnp.maximum(
             small[2 * b, pl.ds(1, 1)], small[2 * b + 1, pl.ds(1, 1)])
 
+    older = sends + bx + bz
+    sends = []
     sends_now = [(dy, dz) for dy in (2, 1, 3, 0) for dz in (2, 1, 3, 0)][:-1]
     back = []
     for k, (dy, dz) in enumerate(sends_now):
@@ -299,18 +300,21 @@
                      device(x, zs[dz], c, ys[dy]))
         out.start()
         sends.append(out)
-        slot = gathered.at[ys[dy], zs[dz]]
-        back.append((slot, s2_send.at[k], s2_recv.at[4 * ys[dy] + zs[dz]]))
-    for slot, send, recv in reversed(back):
-        wait_for(slot, send, recv)
-
-    for zz in range(4):
-        for yy in range(4):
-            slot = 4 * yy + zz
-            for h in range(2):
-                metric_out[pl.ds(8 * yy + 4 * h, 4), pl.ds(zz * LANES, LANES)] = gathered[yy, zz, h]
-            for b in range(RING):
-                z_rows[b, pl.ds(slot, 1)] = gathered[yy, zz, 2, pl.ds(b, 1)]
+        back.append((dy, dz, s2_send.at[k], s2_recv.at[4 * ys[dy] + zs[dz]]))
+    for copy in older:
+        copy.wait_send()
+
+    def place(yy, zz):
+        lanes = pl.ds(pl.multiple_of(LANES * zz, LANES), LANES)
+        rows = pl.ds(pl.multiple_of(8 * yy, 8), 8)
+        metric_out[rows, lanes] = gathered[yy, zz, pl.ds(0, 2)].reshape(8, LANES)
+        for b in range(RING):
+            z_rows[b, pl.ds(4 * yy + zz, 1)] = gathered[yy, zz, 2, pl.ds(b, 1)]
+
+    place(y, z)
+    for dy, dz, send, recv in reversed(back):
+        wait_for(gathered.at[ys[dy], zs[dz]], send, recv)
+        place(ys[dy], zs[dz])
     quarter = iota((16, LANES), 1) >> 5
     blocks = [z_rows[b] for b in range(RING)]
     for zz in range(4):
@@ -321,7 +325,7 @@
             value = jnp.where(quarter == b, moved, value)
         metric_out[pl.ds(32, 16), pl.ds(zz * LANES, LANES)] = value
 
-    for copy in sends + bx + bz:
+    for copy in sends:
         copy.wait_send()
 
 
@@ -391,43 +395,40 @@
     keep = (iota((ROWS, 4 * M), 0) & 3) == (iota((ROWS, 4 * M), 1) & 3)
     areas = ROWS // 4
 
-    def make(r):
-        rows = jnp.dot(repeat, wide[pl.ds(r * areas, areas)], preferred_element_type=jnp.float32)
-        left = jnp.where(keep, rows, 0.0).astype(jnp.bfloat16)
-        lhs[pl.ds(r * ROWS, ROWS)] = left
-        return left
-
-    def part(i, q):
-        some = pl.ds(128 * q, 128)
-        return pltpu.make_async_copy(stage.at[i, some], out.at[some, i], out_sem.at[4 * i + q])
-
-    def step(j, carry, fresh=False):
-        for k in range(2):
-            i = 2 * j + k
-            for r in range(4 * AREAS // ROWS):
-                left = make(r) if fresh and k == 0 else lhs[pl.ds(r * ROWS, ROWS)]
+    half = 4 * AREAS // ROWS // 2
+
+    def part(q, i):
+        some = pl.ds(pl.multiple_of(2 * areas * q, 2 * areas), 2 * areas)
+        return pltpu.make_async_copy(stage.at[some, i], out.at[some, i], out_sem.at[QUADS * q + i])
+
+    def step(q, carry):
+        first = [pl.multiple_of((2 * q + r) * areas, areas) for r in range(2)]
+        for r in range(2):
+            rows = jnp.dot(repeat, wide[pl.ds(first[r], areas)],
+                           preferred_element_type=jnp.float32)
+            lhs[r] = jnp.where(keep, rows, 0.0).astype(jnp.bfloat16)
+        for i in range(QUADS):
+            for r in range(2):
                 parts = []
                 for h in range(2):
-                    acc = jnp.dot(left, slab[i, :, pl.ds(2 * LANES * h, 2 * LANES)],
+                    acc = jnp.dot(lhs[r], slab[i, :, pl.ds(2 * LANES * h, 2 * LANES)],
                                   preferred_element_type=jnp.float32)
                     acc = (acc * (1.0 / (M - 1))).reshape(ROWS // 8, 8, 2 * LANES)
                     both = swap_halves(acc[:, :, :LANES], acc[:, :, LANES:])
                     parts.append(jnp.stack(both, axis=1).reshape(areas, 8, LANES))
                 done = jnp.stack(parts, axis=1).reshape(areas, 16, LANES)
-                stage[i, pl.ds(r * areas, areas)] = done.astype(jnp.bfloat16)
-                if (r + 1) * areas % 128 == 0:
-                    part(i, r * areas // 128).start()
+                stage[pl.ds(first[r], areas), i] = done.astype(jnp.bfloat16)
+            part(q, i).start()
         return carry
 
-    step(0, 0, fresh=True)
-    lax.fori_loop(1, QUADS // 2, step, 0)
-
-    def finish(i, carry):
-        for q in range(4):
-            part(i, q).wait()
+    lax.fori_loop(0, half, step, 0)
+
+    def finish(q, carry):
+        for i in range(QUADS):
+            part(q, i).wait()
         return carry
 
-    lax.fori_loop(0, QUADS, finish, 0)
+    lax.fori_loop(0, half, finish, 0)
 
 
 def product(metric, slab):
@@ -440,8 +441,8 @@
         out_specs=any_space,
         scratch_shapes=[
             pltpu.VMEM((AREAS, 4 * M), jnp.bfloat16),
-            pltpu.VMEM((4 * AREAS, 4 * M), jnp.bfloat16),
-            pltpu.VMEM((QUADS, AREAS, 16, LANES), jnp.bfloat16),
+            pltpu.VMEM((2, ROWS, 4 * M), jnp.bfloat16),
+            pltpu.VMEM((AREAS, QUADS, 16, LANES), jnp.bfloat16),
             dma((32,)),
         ],
         compiler_params=pltpu.CompilerParams(vmem_limit_bytes=32 * 2**20),

time: 39.9 us -> 37.9 us (0.950)
  Pallas kernels: 39.8 us -> 37.8 us
    pallas_call x1, Pallas kernels: 31.8 us -> 30.7 us  [exchange(): pl.pallas_call(exchange_kernel, out_shape=(pltpu.VMEM((M, AREAS), f32), p...]
    pallas_call x1, Pallas kernels: 8.03 us -> 7.11 us  [product(): pl.pallas_call(product_kernel, out_shape=jax.ShapeDtypeStruct((AREAS, QUA...]
where the time goes in v4:
time: 37.9 us; the launch traced here: 37.8 us
  Pallas kernels  37.8 us (100%)
    pallas_call x1, Pallas kernels, exchange(): pl.pallas_call(exchange_kernel, out_shape=(pltpu.VMEM((M, AREAS), f32), p...  30.7 us
    pallas_call x1, Pallas kernels, product(): pl.pallas_call(product_kernel, out_shape=jax.ShapeDtypeStruct((AREAS, QUA...  7.11 us

profile of v4, /device:TPU:1, one launch (start us, length us, event | category | flops | bytes accessed | tf_op | source)
XLA Modules:
  0.0 37.8 jit_solution(13965230873309788003)
XLA Ops:
  0.0 30.7 %exchange.1 = (f32[48,512]{1,0:T(8,128)S(1)}, bf16[8,192,512]{2,1,0:T(8,128)(2,1)S(1)}) custom-call(bf16[48,144,256]{2,1,0:T(8,128)(2,1)} %bitcast.13, s32[1,256]{1,0:T(1,128)} %bitcast.15, s32[1,256]{1,0:T(1,128)} %bitcast.16, s32[16]{0:T(128)} %offsets.1, bf16[48,8,16,128]{3,2,1,0:T(8,128)(2,1)} %bitcast.14), custom_call_target="tpu_custom_call" | custom-call | flops 536870912 | bytes 5242880 | tf_op jit(solution)/shard_map/exchange/pallas_call | solution.py:337
  30.7 7.1 %product.1 = bf16[512,8,16,128]{3,2,1,0:T(8,128)(2,1)} custom-call(f32[48,512]{1,0:T(8,128)S(1)} %get-tuple-element.7.metric, bf16[8,192,512]{2,1,0:T(8,128)(2,1)S(1)} %get-tuple-element.8.slab), custom_call_target="tpu_custom_call" | custom-call | flops 3221225472 | bytes 20971520 | tf_op jit(solution)/shard_map/product/pallas_call | solution.py:437

commit v5 on v4

--- a/solution.py
+++ b/solution.py
@@ -12,7 +12,8 @@
 AREAS = 512
 LANES = 128
 RING = 4
-PAD_X = 160
+ONES = 16
+PAD_X = ONES + T
 ROWS_Z = 80
 PAD_Z = 96
 HALF = 64
@@ -36,22 +37,21 @@
     return jnp.where(low, u, crossed), jnp.where(low, crossed, v)
 
 
-def ramp_metric(summed, steps, offset, ramps):
-    total = jnp.maximum(summed[steps : steps + 1], capacity_floor)
-    power = summed[:steps] / total
+def ramp_metric(power, offset, first, last):
+    steps = power.shape[0]
     wide = jnp.broadcast_to(offset, power.shape).astype(jnp.int32)
     later = power
     for bit in (1, 2, 4, 8):
         later = jnp.where((wide & bit) != 0, pltpu.roll(later, steps - bit, 0), later)
     row = iota(power.shape, 0)
-    return jnp.max(jnp.where(row < ramps, later - power, -3e38), axis=0, keepdims=True)
+    inside = (row >= first) & (row < last)
+    return jnp.max(jnp.where(inside, later - power, -3e38), axis=0, keepdims=True)
 
 
 STEP = (0, 0, 1, 1, 3, 3, 2, 2)
 BACK = (0, 1, 4, 5, 2, 3, 6, 7)
 ORDER = (6, 7, 2, 4, 3, 5, 1)
-FIRST = 96
-HALVES = (pl.ds(0, FIRST), pl.ds(FIRST, T - FIRST))
+STARTS, ROWS_X = (0, 96), (96, 48)
 
 
 def exchange_kernel(
@@ -59,10 +59,10 @@
     area_in, capacity_in, offsets_in,
     facts_x, facts_z, got_x, got_z, weight_x, weight_z,
     part_x, part_z, sum_x, sum_z, off_x, off_z,
-    small, gathered, z_rows, st,
+    metrics, st,
     local_sem, fx_send, fx_recv, fz_send, fz_recv, x_send, x_recv, z_send, z_recv,
     bx_send, bx_recv, bz_send, bz_recv,
-    s1_send, s1_recv, s2_send, s2_recv,
+    all_send, all_recv,
 ):
     g = lax.axis_index("grid")
     y = lax.axis_index("lev")
@@ -111,7 +111,7 @@
         greet(device(x, z, c, ys[d]))
 
     def x_slot(i, half):
-        return got_x.at[HALVES[half], pl.ds(F * i, F)]
+        return got_x.at[pl.ds(ONES + STARTS[half], ROWS_X[half]), pl.ds(F * i, F)]
 
     def z_slot(i):
         return got_z.at[pl.ds(0, ROWS_Z), pl.ds(F * i, F)]
@@ -127,7 +127,7 @@
         pltpu.make_async_copy(capacity, capacity_in, local_sem.at[1]),
         pltpu.make_async_copy(offsets, offsets_in, local_sem.at[2]),
         pltpu.make_async_copy(z_tile(z, c), z_slot(0), local_sem.at[3]),
-        pltpu.make_async_copy(x_tile(x, c), got_x.at[pl.ds(0, T), pl.ds(0, F)], local_sem.at[4]),
+        pltpu.make_async_copy(x_tile(x, c), got_x.at[pl.ds(ONES, T), pl.ds(0, F)], local_sem.at[4]),
         pltpu.make_async_copy(state, st, local_sem.at[5]),
     ]
     for copy in local:
@@ -146,7 +146,7 @@
 
     def x_copy(i, half):
         xx, cc = x_peers[i]
-        return remote(x_tile(xx, cc).at[HALVES[half]], x_slot(BACK[i], half),
+        return remote(x_tile(xx, cc).at[pl.ds(STARTS[half], ROWS_X[half])], x_slot(BACK[i], half),
                       x_send.at[half, i], x_recv.at[half, BACK[i]], device(xx, z, cc, y))
 
     def z_copy(i):
@@ -185,7 +185,7 @@
     for i in ORDER:
         start(x_copy(i, 1))
 
-    got_x[pl.ds(T, 16)] = jnp.ones((16, 8 * F), jnp.bfloat16)
+    got_x[pl.ds(0, ONES)] = jnp.ones((ONES, 8 * F), jnp.bfloat16)
     got_z[pl.ds(ROWS_Z, 16)] = jnp.ones((16, 8 * F), jnp.bfloat16)
     off_x[...] = jnp.zeros_like(off_x)
     off_z[...] = jnp.zeros_like(off_z)
@@ -212,6 +212,30 @@
         return lax.dot_general(values, weights, (((1,), (1,)), ((), ())),
                                preferred_element_type=jnp.float32)
 
+    bz, bx = [], ([], [])
+
+    def sum_x_half(half, first, count, skip):
+        keep = count - skip
+        rows = pl.ds(first + skip - 8, keep)
+        for pair in ((2, 1), (3, 0)):
+            chosen = jnp.concatenate(
+                [weight_x[pl.ds(pl.multiple_of(LANES * zs[d], LANES), LANES)] for d in pair],
+                axis=0)
+            value = sum_up(got_x[pl.ds(first, count)], chosen)
+            for k, d in enumerate(pair):
+                part_x[zs[d], rows] = value[skip:, k * LANES : (k + 1) * LANES]
+                if d > 0:
+                    copy = remote(part_x.at[zs[d], rows], sum_x.at[3 - d, rows],
+                                  bx_send.at[half, d - 1], bx_recv.at[half, 3 - d],
+                                  device(x, zs[d], c, y))
+                    copy.start()
+                    bx[half].append(copy)
+
+    local[4].wait()
+    for i in range(1, 8):
+        wait_for(x_slot(i, 0), x_send.at[0, i], x_recv.at[0, i])
+    sum_x_half(0, 0, ONES + ROWS_X[0], 8)
+
     local[3].wait()
     for i in range(1, 8):
         wait_for(z_slot(i), z_send.at[i], z_recv.at[i])
@@ -219,33 +243,57 @@
         value = sum_up(got_z[...], weight_z[pl.ds(2 * LANES * h, 2 * LANES)])
         for b in range(2):
             part_z[2 * h + b] = value[:KEEP_Z, b * LANES : (b + 1) * LANES]
-    local[4].wait()
-    bz, bx = [], []
-
-    def part_copy(d, half, first, count):
-        rows = pl.ds(first, count)
-        return remote(part_x.at[zs[d], rows], sum_x.at[3 - d, rows], bx_send.at[half, d - 1],
-                      bx_recv.at[half, 3 - d], device(x, zs[d], c, y))
-
-    for half, (first, count, keep) in enumerate(
-            ((0, FIRST, FIRST), (FIRST, PAD_X - FIRST, KEEP_X - FIRST))):
-        for i in range(1, 8):
-            wait_for(x_slot(i, half), x_send.at[half, i], x_recv.at[half, i])
-        if half == 1:
-            for d in (2, 1, 3):
-                bz.append(remote(part_z.at[xs[d]], sum_z.at[3 - d], bz_send.at[d - 1], bz_recv.at[3 - d],
-                                 device(xs[d], z, c, y)))
-                bz[-1].start()
-        for pair in ((2, 1), (3, 0)):
-            chosen = jnp.concatenate(
-                [weight_x[pl.ds(pl.multiple_of(LANES * zs[d], LANES), LANES)] for d in pair],
-                axis=0)
-            value = sum_up(got_x[pl.ds(first, count)], chosen)
-            for k, d in enumerate(pair):
-                part_x[zs[d], pl.ds(first, keep)] = value[:keep, k * LANES : (k + 1) * LANES]
-                if d > 0:
-                    bx.append(part_copy(d, half, first, keep))
-                    bx[-1].start()
+
+    for i in range(1, 8):
+        wait_for(x_slot(i, 1), x_send.at[1, i], x_recv.at[1, i])
+    for d in (2, 1, 3):
+        copy = remote(part_z.at[xs[d]], sum_z.at[3 - d], bz_send.at[d - 1], bz_recv.at[3 - d],
+                      device(xs[d], z, c, y))
+        copy.start()
+        bz.append(copy)
+    sum_x_half(1, ONES + ROWS_X[0], ROWS_X[1], 0)
+
+    def whole(copies, own, others, rows):
+        for copy in copies:
+            copy.wait_recv()
+        total = own[rows]
+        for k in range(3):
+            total = total + others[k, rows]
+        return total
+
+    spot = (4 * y + z) * 8 + mine_x
+
+    early_rows, late_rows = pl.ds(0, 8 + ROWS_X[0]), pl.ds(8 + ROWS_X[0], ROWS_X[1])
+    first = whole(bx[0], part_x.at[z], sum_x, early_rows)
+    total = jnp.maximum(first[:1], capacity_floor)
+    power = first[8:] / total
+    early = ramp_metric(power, off_x[...], 0, 84)
+    last = whole(bz, part_z.at[x], sum_z, pl.ds(0, KEEP_Z))
+    metrics[spot, pl.ds(1, 1)] = ramp_metric(
+        last[:ROWS_Z] / jnp.maximum(last[ROWS_Z : ROWS_Z + 1], capacity_floor),
+        off_z[...], 0, RAMPS_Z)
+    last = whole(bx[1], part_x.at[z], sum_x, late_rows)
+    power = jnp.concatenate([power[80:], last / total], axis=0)
+    late = ramp_metric(power, off_x[...], 4, 52)
+    metrics[spot, pl.ds(0, 1)] = jnp.maximum(early, late)
+
+    mine = metrics.at[spot]
+
+    def broadcast(xx, zz, cc, yy):
+        remote(mine, mine, all_send, all_recv, device(xx, zz, cc, yy)).start()
+
+    @loop(0, 15)
+    def _(k):
+        step = 1 + lax.rem(k + 9, 15)
+        yy, zz = lax.rem(y + lax.div(step, 4), 4), lax.rem(z + lax.rem(step, 4), 4)
+        for i in (6, 7, 2, 3, 4, 5, 0, 1):
+            xx, cc = x_peers[i]
+            broadcast(xx, zz, cc, yy)
+
+    for i in ORDER:
+        xx, cc = x_peers[i]
+        broadcast(xx, z, cc, y)
+
     local[5].wait()
 
     @loop(0, QUADS)
@@ -259,64 +307,21 @@
                 slab_out[i, :, pl.ds((2 * h + k) * LANES, LANES)] = (
                     both[k].reshape(4 * M, LANES).astype(jnp.bfloat16))
 
-    for copy in bz:
-        copy.wait_recv()
-    summed = part_z[x] + sum_z[0] + sum_z[1] + sum_z[2]
-    small[mine_x, pl.ds(1, 1)] = ramp_metric(summed, ROWS_Z, off_z[...], RAMPS_Z)
-
-    for copy in bx:
-        copy.wait_recv()
-
-    summed = part_x[z] + sum_x[0] + sum_x[1] + sum_x[2]
-    small[mine_x, pl.ds(0, 1)] = ramp_metric(summed, T, off_x[...], RAMPS)
-
-    def swap(ref, slot, far, send_sem, recv_sem, to):
-        copy = remote(ref.at[slot], ref.at[slot], send_sem, recv_sem.at[slot], to)
-        copy.start()
-        sends.append(copy)
-        return remote(ref.at[far], ref.at[far], send_sem, recv_sem.at[far], to)
-
-    back = []
-    for i in ORDER:
-        xx, cc = x_peers[i]
-        back.append(swap(small, mine_x, 2 * xx + cc, s1_send.at[i], s1_recv,
-                         device(xx, z, cc, y)))
-    for copy in reversed(back):
-        copy.wait_recv()
-
-    joined = gathered.at[y, z]
-    for s in range(8):
-        joined[s // 4, pl.ds(s % 4, 1)] = small[s, pl.ds(0, 1)]
-    for b in range(RING):
-        joined[2, pl.ds(b, 1)] = jnp.maximum(
-            small[2 * b, pl.ds(1, 1)], small[2 * b + 1, pl.ds(1, 1)])
-
-    older = sends + bx + bz
-    sends = []
-    sends_now = [(dy, dz) for dy in (2, 1, 3, 0) for dz in (2, 1, 3, 0)][:-1]
-    back = []
-    for k, (dy, dz) in enumerate(sends_now):
-        out = remote(joined, joined, s2_send.at[k], s2_recv.at[4 * y + z],
-                     device(x, zs[dz], c, ys[dy]))
-        out.start()
-        sends.append(out)
-        back.append((dy, dz, s2_send.at[k], s2_recv.at[4 * ys[dy] + zs[dz]]))
-    for copy in older:
+    for copy in sends + bx[0] + bx[1] + bz:
         copy.wait_send()
 
-    def place(yy, zz):
-        lanes = pl.ds(pl.multiple_of(LANES * zz, LANES), LANES)
-        rows = pl.ds(pl.multiple_of(8 * yy, 8), 8)
-        metric_out[rows, lanes] = gathered[yy, zz, pl.ds(0, 2)].reshape(8, LANES)
-        for b in range(RING):
-            z_rows[b, pl.ds(4 * yy + zz, 1)] = gathered[yy, zz, 2, pl.ds(b, 1)]
-
-    place(y, z)
-    for dy, dz, send, recv in reversed(back):
-        wait_for(gathered.at[ys[dy], zs[dz]], send, recv)
-        place(ys[dy], zs[dz])
+    others = metrics.at[pl.ds(0, 127)]
+    everything = remote(others, others, all_send, all_recv, sibling)
+    everything.wait_recv()
+
+    rows = metrics.reshape(256, LANES)
+    for yy in range(4):
+        for zz in range(4):
+            metric_out[pl.ds(8 * yy, 8), pl.ds(LANES * zz, LANES)] = (
+                rows[pl.ds(16 * (4 * yy + zz), 8, stride=2)])
     quarter = iota((16, LANES), 1) >> 5
-    blocks = [z_rows[b] for b in range(RING)]
+    blocks = [jnp.maximum(rows[pl.ds(4 * b + 1, 16, stride=16)], rows[pl.ds(4 * b + 3, 16, stride=16)])
+              for b in range(RING)]
     for zz in range(4):
         value = jnp.zeros((16, LANES), jnp.float32)
         for b in range(RING):
@@ -325,8 +330,7 @@
             value = jnp.where(quarter == b, moved, value)
         metric_out[pl.ds(32, 16), pl.ds(zz * LANES, LANES)] = value
 
-    for copy in sends:
-        copy.wait_send()
+    everything.wait_send()
 
 
 def exchange(tiles, farm_area, capacity, offsets, state):
@@ -358,14 +362,12 @@
             pltpu.VMEM((3, KEEP_Z, LANES), f32),
             pltpu.VMEM((1, LANES), f32),
             pltpu.VMEM((1, LANES), f32),
-            pltpu.VMEM((8, 2, LANES), f32),
-            pltpu.VMEM((4, 4, 3, 4, LANES), f32),
-            pltpu.VMEM((RING, 16, LANES), f32),
+            pltpu.VMEM((128, 2, LANES), f32),
             pltpu.VMEM((M, QUADS, 16, LANES), bf16),
             dma((6,)), dma((8,)), dma((8,)), dma((8,)), dma((8,)),
             dma((2, 8)), dma((2, 8)), dma((8,)), dma((8,)),
             dma((2, 3)), dma((2, 3)), dma((3,)), dma((3,)),
-            dma((8,)), dma((8,)), dma((16,)), dma((16,)),
+            dma, dma,
         ],
         compiler_params=pltpu.CompilerParams(
             collective_id=0, has_side_effects=True, vmem_limit_bytes=60 * 2**20),

time: 37.9 us -> 37.3 us (0.984)
  Pallas kernels: 37.8 us -> 37.2 us
    pallas_call x1, Pallas kernels: 30.7 us -> 30.1 us  [exchange(): pl.pallas_call(exchange_kernel, out_shape=(pltpu.VMEM((M, AREAS), f32), p...]
where the time goes in v5:
time: 37.3 us; the launch traced here: 37.2 us
  Pallas kernels  37.2 us (100%)
    pallas_call x1, Pallas kernels, exchange(): pl.pallas_call(exchange_kernel, out_shape=(pltpu.VMEM((M, AREAS), f32), p...  30.1 us
    pallas_call x1, Pallas kernels, product(): pl.pallas_call(product_kernel, out_shape=jax.ShapeDtypeStruct((AREAS, QUA...  7.11 us

profile of v5, /device:TPU:1, one launch (start us, length us, event | category | flops | bytes accessed | tf_op | source)
XLA Modules:
  0.0 37.2 jit_solution(15805196037080200919)
XLA Ops:
  0.0 30.1 %exchange.1 = (f32[48,512]{1,0:T(8,128)S(1)}, bf16[8,192,512]{2,1,0:T(8,128)(2,1)S(1)}) custom-call(bf16[48,144,256]{2,1,0:T(8,128)(2,1)} %bitcast.13, s32[1,256]{1,0:T(1,128)} %bitcast.15, s32[1,256]{1,0:T(1,128)} %bitcast.16, s32[16]{0:T(128)} %offsets.1, bf16[48,8,16,128]{3,2,1,0:T(8,128)(2,1)} %bitcast.14), custom_call_target="tpu_custom_call" | custom-call | flops 536870912 | bytes 5242880 | tf_op jit(solution)/shard_map/exchange/pallas_call | solution.py:341
  30.1 7.1 %product.1 = bf16[512,8,16,128]{3,2,1,0:T(8,128)(2,1)} custom-call(f32[48,512]{1,0:T(8,128)S(1)} %get-tuple-element.7.metric, bf16[8,192,512]{2,1,0:T(8,128)(2,1)S(1)} %get-tuple-element.8.slab), custom_call_target="tpu_custom_call" | custom-call | flops 3221225472 | bytes 20971520 | tf_op jit(solution)/shard_map/product/pallas_call | solution.py:439

commit v6 on v5

--- a/solution.py
+++ b/solution.py
@@ -51,6 +51,7 @@
 STEP = (0, 0, 1, 1, 3, 3, 2, 2)
 BACK = (0, 1, 4, 5, 2, 3, 6, 7)
 ORDER = (6, 7, 2, 4, 3, 5, 1)
+NEAR = 6
 STARTS, ROWS_X = (0, 96), (96, 48)
 
 
@@ -182,7 +183,7 @@
     for i in ORDER[2:]:
         start(x_copy(i, 0), z_copy(i))
 
-    for i in ORDER:
+    for i in ORDER[2:] + ORDER[:2]:
         start(x_copy(i, 1))
 
     got_x[pl.ds(0, ONES)] = jnp.ones((ONES, 8 * F), jnp.bfloat16)
@@ -214,27 +215,31 @@
 
     bz, bx = [], ([], [])
 
-    def sum_x_half(half, first, count, skip):
-        keep = count - skip
-        rows = pl.ds(first + skip - 8, keep)
-        for pair in ((2, 1), (3, 0)):
-            chosen = jnp.concatenate(
-                [weight_x[pl.ds(pl.multiple_of(LANES * zs[d], LANES), LANES)] for d in pair],
-                axis=0)
-            value = sum_up(got_x[pl.ds(first, count)], chosen)
-            for k, d in enumerate(pair):
-                part_x[zs[d], rows] = value[skip:, k * LANES : (k + 1) * LANES]
-                if d > 0:
-                    copy = remote(part_x.at[zs[d], rows], sum_x.at[3 - d, rows],
-                                  bx_send.at[half, d - 1], bx_recv.at[half, 3 - d],
-                                  device(x, zs[d], c, y))
-                    copy.start()
-                    bx[half].append(copy)
-
+    pairs = ((2, 1), (3, 0))
+    near, far = pl.ds(0, NEAR * F), pl.ds(NEAR * F, (8 - NEAR) * F)
+
+    def dot_x(first, count, pair, columns):
+        chosen = jnp.concatenate(
+            [weight_x[pl.ds(pl.multiple_of(LANES * zs[d], LANES), LANES), columns] for d in pair],
+            axis=0)
+        return sum_up(got_x[pl.ds(first, count), columns], chosen)
+
+    def leave(half, pair, rows, value):
+        for k, d in enumerate(pair):
+            part_x[zs[d], rows] = value[:, k * LANES : (k + 1) * LANES]
+            if d > 0:
+                copy = remote(part_x.at[zs[d], rows], sum_x.at[3 - d, rows],
+                              bx_send.at[half, d - 1], bx_recv.at[half, 3 - d],
+                              device(x, zs[d], c, y))
+                copy.start()
+                bx[half].append(copy)
+
+    early_rows, late_rows = pl.ds(0, 8 + ROWS_X[0]), pl.ds(8 + ROWS_X[0], ROWS_X[1])
     local[4].wait()
     for i in range(1, 8):
         wait_for(x_slot(i, 0), x_send.at[0, i], x_recv.at[0, i])
-    sum_x_half(0, 0, ONES + ROWS_X[0], 8)
+    for pair in pairs:
+        leave(0, pair, early_rows, dot_x(0, ONES + ROWS_X[0], pair, pl.ds(0, 8 * F))[8:])
 
     local[3].wait()
     for i in range(1, 8):
@@ -243,15 +248,19 @@
         value = sum_up(got_z[...], weight_z[pl.ds(2 * LANES * h, 2 * LANES)])
         for b in range(2):
             part_z[2 * h + b] = value[:KEEP_Z, b * LANES : (b + 1) * LANES]
-
-    for i in range(1, 8):
-        wait_for(x_slot(i, 1), x_send.at[1, i], x_recv.at[1, i])
     for d in (2, 1, 3):
         copy = remote(part_z.at[xs[d]], sum_z.at[3 - d], bz_send.at[d - 1], bz_recv.at[3 - d],
                       device(xs[d], z, c, y))
         copy.start()
         bz.append(copy)
-    sum_x_half(1, ONES + ROWS_X[0], ROWS_X[1], 0)
+
+    for i in range(1, NEAR):
+        wait_for(x_slot(i, 1), x_send.at[1, i], x_recv.at[1, i])
+    values = [dot_x(ONES + ROWS_X[0], ROWS_X[1], pair, near) for pair in pairs]
+    for i in range(NEAR, 8):
+        wait_for(x_slot(i, 1), x_send.at[1, i], x_recv.at[1, i])
+    for pair, value in zip(pairs, values):
+        leave(1, pair, late_rows, value + dot_x(ONES + ROWS_X[0], ROWS_X[1], pair, far))
 
     def whole(copies, own, others, rows):
         for copy in copies:
@@ -263,7 +272,6 @@
 
     spot = (4 * y + z) * 8 + mine_x
 
-    early_rows, late_rows = pl.ds(0, 8 + ROWS_X[0]), pl.ds(8 + ROWS_X[0], ROWS_X[1])
     first = whole(bx[0], part_x.at[z], sum_x, early_rows)
     total = jnp.maximum(first[:1], capacity_floor)
     power = first[8:] / total
@@ -420,7 +428,7 @@
                     parts.append(jnp.stack(both, axis=1).reshape(areas, 8, LANES))
                 done = jnp.stack(parts, axis=1).reshape(areas, 16, LANES)
                 stage[pl.ds(first[r], areas), i] = done.astype(jnp.bfloat16)
-            part(q, i).start()
+            part(q, i).start(priority=i % 2)
         return carry
 
     lax.fori_loop(0, half, step, 0)

time: 37.3 us -> 36.8 us (0.987)
  Pallas kernels: 37.2 us -> 36.7 us
    pallas_call x1, Pallas kernels: 30.1 us -> 29.6 us  [exchange(): pl.pallas_call(exchange_kernel, out_shape=(pltpu.VMEM((M, AREAS), f32), p...]
where the time goes in v6:
time: 36.8 us; the launch traced here: 36.7 us
  Pallas kernels  36.7 us (100%)
    pallas_call x1, Pallas kernels, exchange(): pl.pallas_call(exchange_kernel, out_shape=(pltpu.VMEM((M, AREAS), f32), p...  29.6 us
    pallas_call x1, Pallas kernels, product(): pl.pallas_call(product_kernel, out_shape=jax.ShapeDtypeStruct((AREAS, QUA...  7.11 us

profile of v6, /device:TPU:1, one launch (start us, length us, event | category | flops | bytes accessed | tf_op | source)
XLA Modules:
  0.0 36.7 jit_solution(7877274676388358789)
XLA Ops:
  0.0 29.6 %exchange.1 = (f32[48,512]{1,0:T(8,128)S(1)}, bf16[8,192,512]{2,1,0:T(8,128)(2,1)S(1)}) custom-call(bf16[48,144,256]{2,1,0:T(8,128)(2,1)} %bitcast.13, s32[1,256]{1,0:T(1,128)} %bitcast.15, s32[1,256]{1,0:T(1,128)} %bitcast.16, s32[16]{0:T(128)} %offsets.1, bf16[48,8,16,128]{3,2,1,0:T(8,128)(2,1)} %bitcast.14), custom_call_target="tpu_custom_call" | custom-call | flops 536870912 | bytes 5242880 | tf_op jit(solution)/shard_map/exchange/pallas_call | solution.py:349
  29.6 7.1 %product.1 = bf16[512,8,16,128]{3,2,1,0:T(8,128)(2,1)} custom-call(f32[48,512]{1,0:T(8,128)S(1)} %get-tuple-element.7.metric, bf16[8,192,512]{2,1,0:T(8,128)(2,1)S(1)} %get-tuple-element.8.slab), custom_call_target="tpu_custom_call" | custom-call | flops 3221225472 | bytes 20971520 | tf_op jit(solution)/shard_map/product/pallas_call | solution.py:447

commit v7 on v6

--- a/solution.py
+++ b/solution.py
@@ -59,7 +59,7 @@
     tiles, farm_area, capacity, offsets, state, metric_out, slab_out,
     area_in, capacity_in, offsets_in,
     facts_x, facts_z, got_x, got_z, weight_x, weight_z,
-    part_x, part_z, sum_x, sum_z, off_x, off_z,
+    part_x, part_z, sum_x, sum_z, near_x, off_x, off_z,
     metrics, st,
     local_sem, fx_send, fx_recv, fz_send, fz_recv, x_send, x_recv, z_send, z_recv,
     bx_send, bx_recv, bz_send, bz_recv,
@@ -133,8 +133,6 @@
     ]
     for copy in local:
         copy.start()
-    pl.semaphore_wait(barrier, 16)
-
     def fx_copy(i):
         xx, cc = x_peers[i]
         return remote(facts_x.at[0], facts_x.at[BACK[i]], fx_send.at[i], fx_recv.at[BACK[i]],
@@ -162,7 +160,6 @@
             copy.start()
             sends.append(copy)
 
-    start(x_copy(6, 0), x_copy(7, 0), z_copy(6), z_copy(7))
     for copy in local[:3]:
         copy.wait()
 
@@ -178,11 +175,11 @@
             [ids, capacity_in[...], placed, jnp.zeros((1, F), jnp.int32)], axis=0)
         facts[0] = rows.astype(jnp.float32)
 
+    pl.semaphore_wait(barrier, 16)
     for i in ORDER:
-        start(fz_copy(i), fx_copy(i))
-    for i in ORDER[2:]:
+        start(fx_copy(i), fz_copy(i))
+    for i in ORDER:
         start(x_copy(i, 0), z_copy(i))
-
     for i in ORDER[2:] + ORDER[:2]:
         start(x_copy(i, 1))
 
@@ -213,33 +210,40 @@
         return lax.dot_general(values, weights, (((1,), (1,)), ((), ())),
                                preferred_element_type=jnp.float32)
 
-    bz, bx = [], ([], [])
-
-    pairs = ((2, 1), (3, 0))
+    bz = []
+
     near, far = pl.ds(0, NEAR * F), pl.ds(NEAR * F, (8 - NEAR) * F)
 
-    def dot_x(first, count, pair, columns):
+    def block_pair(p):
+        return lax.rem(z + 2 + p, 4), lax.rem(z + 1 + 3 * p, 4)
+
+    def dot_x(first, count, p, columns):
         chosen = jnp.concatenate(
-            [weight_x[pl.ds(pl.multiple_of(LANES * zs[d], LANES), LANES), columns] for d in pair],
-            axis=0)
+            [weight_x[pl.ds(pl.multiple_of(LANES * zz, LANES), LANES), columns]
+             for zz in block_pair(p)], axis=0)
         return sum_up(got_x[pl.ds(first, count), columns], chosen)
 
-    def leave(half, pair, rows, value):
-        for k, d in enumerate(pair):
-            part_x[zs[d], rows] = value[:, k * LANES : (k + 1) * LANES]
-            if d > 0:
-                copy = remote(part_x.at[zs[d], rows], sum_x.at[3 - d, rows],
-                              bx_send.at[half, d - 1], bx_recv.at[half, 3 - d],
-                              device(x, zs[d], c, y))
-                copy.start()
-                bx[half].append(copy)
+    def sum_copy(half, rows, d, zz):
+        return remote(part_x.at[zz, rows], sum_x.at[3 - d, rows], bx_send.at[half, d - 1],
+                      bx_recv.at[half, 3 - d], device(x, zz, c, y))
+
+    def leave(half, rows, p, value):
+        for k, zz in enumerate(block_pair(p)):
+            part_x[zz, rows] = value[:, k * LANES : (k + 1) * LANES]
+        sum_copy(half, rows, 2 + p, block_pair(p)[0]).start()
+
+        @pl.when(p == 0)
+        def _():
+            sum_copy(half, rows, 1, zs[1]).start()
 
     early_rows, late_rows = pl.ds(0, 8 + ROWS_X[0]), pl.ds(8 + ROWS_X[0], ROWS_X[1])
     local[4].wait()
     for i in range(1, 8):
         wait_for(x_slot(i, 0), x_send.at[0, i], x_recv.at[0, i])
-    for pair in pairs:
-        leave(0, pair, early_rows, dot_x(0, ONES + ROWS_X[0], pair, pl.ds(0, 8 * F))[8:])
+
+    @loop(0, 2)
+    def _(p):
+        leave(0, early_rows, p, dot_x(0, ONES + ROWS_X[0], p, pl.ds(0, 8 * F))[8:])
 
     local[3].wait()
     for i in range(1, 8):
@@ -256,11 +260,20 @@
 
     for i in range(1, NEAR):
         wait_for(x_slot(i, 1), x_send.at[1, i], x_recv.at[1, i])
-    values = [dot_x(ONES + ROWS_X[0], ROWS_X[1], pair, near) for pair in pairs]
+
+    @loop(0, 2)
+    def _(p):
+        near_x[p] = dot_x(ONES + ROWS_X[0], ROWS_X[1], p, near)
+
     for i in range(NEAR, 8):
         wait_for(x_slot(i, 1), x_send.at[1, i], x_recv.at[1, i])
-    for pair, value in zip(pairs, values):
-        leave(1, pair, late_rows, value + dot_x(ONES + ROWS_X[0], ROWS_X[1], pair, far))
+
+    @loop(0, 2)
+    def _(p):
+        leave(1, late_rows, p, near_x[p] + dot_x(ONES + ROWS_X[0], ROWS_X[1], p, far))
+
+    bx = [[sum_copy(half, rows, d, zs[d]) for d in range(1, 4)]
+          for half, rows in ((0, early_rows), (1, late_rows))]
 
     def whole(copies, own, others, rows):
         for copy in copies:
@@ -368,6 +381,7 @@
             pltpu.VMEM((RING, KEEP_Z, LANES), f32),
             pltpu.VMEM((3, KEEP_X, LANES), f32),
             pltpu.VMEM((3, KEEP_Z, LANES), f32),
+            pltpu.VMEM((2, ROWS_X[1], 2 * LANES), f32),
             pltpu.VMEM((1, LANES), f32),
             pltpu.VMEM((1, LANES), f32),
             pltpu.VMEM((128, 2, LANES), f32),

time: 36.8 us -> 36.5 us (level)
  no operation moved by 1% of the time
where the time goes in v7:
time: 36.5 us; the launch traced here: 36.4 us
  Pallas kernels  36.4 us (100%)
    pallas_call x1, Pallas kernels, exchange(): pl.pallas_call(exchange_kernel, out_shape=(pltpu.VMEM((M, AREAS), f32), p...  29.3 us
    pallas_call x1, Pallas kernels, product(): pl.pallas_call(product_kernel, out_shape=jax.ShapeDtypeStruct((AREAS, QUA...  7.11 us

profile of v7, /device:TPU:1, one launch (start us, length us, event | category | flops | bytes accessed | tf_op | source)
XLA Modules:
  0.0 36.4 jit_solution(2793526464176854087)
XLA Ops:
  0.0 29.3 %exchange.1 = (f32[48,512]{1,0:T(8,128)S(1)}, bf16[8,192,512]{2,1,0:T(8,128)(2,1)S(1)}) custom-call(bf16[48,144,256]{2,1,0:T(8,128)(2,1)} %bitcast.13, s32[1,256]{1,0:T(1,128)} %bitcast.15, s32[1,256]{1,0:T(1,128)} %bitcast.16, s32[16]{0:T(128)} %offsets.1, bf16[48,8,16,128]{3,2,1,0:T(8,128)(2,1)} %bitcast.14), custom_call_target="tpu_custom_call" | custom-call | flops 536870912 | bytes 5242880 | tf_op jit(solution)/shard_map/exchange/pallas_call | solution.py:362
  29.3 7.1 %product.1 = bf16[512,8,16,128]{3,2,1,0:T(8,128)(2,1)} custom-call(f32[48,512]{1,0:T(8,128)S(1)} %get-tuple-element.7.metric, bf16[8,192,512]{2,1,0:T(8,128)(2,1)S(1)} %get-tuple-element.8.slab), custom_call_target="tpu_custom_call" | custom-call | flops 3221225472 | bytes 20971520 | tf_op jit(solution)/shard_map/product/pallas_call | solution.py:461

commit v8 on v7

--- a/solution.py
+++ b/solution.py
@@ -60,10 +60,10 @@
     area_in, capacity_in, offsets_in,
     facts_x, facts_z, got_x, got_z, weight_x, weight_z,
     part_x, part_z, sum_x, sum_z, near_x, off_x, off_z,
-    metrics, st,
+    metric_x, metric_z, st,
     local_sem, fx_send, fx_recv, fz_send, fz_recv, x_send, x_recv, z_send, z_recv,
     bx_send, bx_recv, bz_send, bz_recv,
-    all_send, all_recv,
+    x_sems, z_sems,
 ):
     g = lax.axis_index("grid")
     y = lax.axis_index("lev")
@@ -285,35 +285,40 @@
 
     spot = (4 * y + z) * 8 + mine_x
 
+    def broadcast(metrics, sem):
+        mine = metrics.at[spot]
+
+        def one(xx, zz, cc, yy):
+            remote(mine, mine, sem.at[0], sem.at[1], device(xx, zz, cc, yy)).start()
+
+        @loop(0, 15)
+        def _(k):
+            step = 1 + lax.rem(k + 9, 15)
+            yy, zz = lax.rem(y + lax.div(step, 4), 4), lax.rem(z + lax.rem(step, 4), 4)
+            for i in (6, 7, 2, 3, 4, 5, 0, 1):
+                xx, cc = x_peers[i]
+                one(xx, zz, cc, yy)
+
+        for i in ORDER:
+            xx, cc = x_peers[i]
+            one(xx, z, cc, y)
+        others = metrics.at[pl.ds(0, 127)]
+        return remote(others, others, sem.at[0], sem.at[1], sibling)
+
+    last = whole(bz, part_z.at[x], sum_z, pl.ds(0, KEEP_Z))
+    metric_z[spot] = ramp_metric(
+        last[:ROWS_Z] / jnp.maximum(last[ROWS_Z : ROWS_Z + 1], capacity_floor),
+        off_z[...], 0, RAMPS_Z)
+    all_z = broadcast(metric_z, z_sems)
     first = whole(bx[0], part_x.at[z], sum_x, early_rows)
     total = jnp.maximum(first[:1], capacity_floor)
     power = first[8:] / total
     early = ramp_metric(power, off_x[...], 0, 84)
-    last = whole(bz, part_z.at[x], sum_z, pl.ds(0, KEEP_Z))
-    metrics[spot, pl.ds(1, 1)] = ramp_metric(
-        last[:ROWS_Z] / jnp.maximum(last[ROWS_Z : ROWS_Z + 1], capacity_floor),
-        off_z[...], 0, RAMPS_Z)
     last = whole(bx[1], part_x.at[z], sum_x, late_rows)
     power = jnp.concatenate([power[80:], last / total], axis=0)
     late = ramp_metric(power, off_x[...], 4, 52)
-    metrics[spot, pl.ds(0, 1)] = jnp.maximum(early, late)
-
-    mine = metrics.at[spot]
-
-    def broadcast(xx, zz, cc, yy):
-        remote(mine, mine, all_send, all_recv, device(xx, zz, cc, yy)).start()
-
-    @loop(0, 15)
-    def _(k):
-        step = 1 + lax.rem(k + 9, 15)
-        yy, zz = lax.rem(y + lax.div(step, 4), 4), lax.rem(z + lax.rem(step, 4), 4)
-        for i in (6, 7, 2, 3, 4, 5, 0, 1):
-            xx, cc = x_peers[i]
-            broadcast(xx, zz, cc, yy)
-
-    for i in ORDER:
-        xx, cc = x_peers[i]
-        broadcast(xx, z, cc, y)
+    metric_x[spot] = jnp.maximum(early, late)
+    all_x = broadcast(metric_x, x_sems)
 
     local[5].wait()
 
@@ -331,17 +336,17 @@
     for copy in sends + bx[0] + bx[1] + bz:
         copy.wait_send()
 
-    others = metrics.at[pl.ds(0, 127)]
-    everything = remote(others, others, all_send, all_recv, sibling)
-    everything.wait_recv()
-
-    rows = metrics.reshape(256, LANES)
+    all_z.wait_recv()
+    all_x.wait_recv()
+
+    rows = metric_x.reshape(128, LANES)
     for yy in range(4):
         for zz in range(4):
             metric_out[pl.ds(8 * yy, 8), pl.ds(LANES * zz, LANES)] = (
-                rows[pl.ds(16 * (4 * yy + zz), 8, stride=2)])
+                rows[pl.ds(8 * (4 * yy + zz), 8)])
+    rows = metric_z.reshape(128, LANES)
     quarter = iota((16, LANES), 1) >> 5
-    blocks = [jnp.maximum(rows[pl.ds(4 * b + 1, 16, stride=16)], rows[pl.ds(4 * b + 3, 16, stride=16)])
+    blocks = [jnp.maximum(rows[pl.ds(2 * b, 16, stride=8)], rows[pl.ds(2 * b + 1, 16, stride=8)])
               for b in range(RING)]
     for zz in range(4):
         value = jnp.zeros((16, LANES), jnp.float32)
@@ -351,7 +356,8 @@
             value = jnp.where(quarter == b, moved, value)
         metric_out[pl.ds(32, 16), pl.ds(zz * LANES, LANES)] = value
 
-    everything.wait_send()
+    all_z.wait_send()
+    all_x.wait_send()
 
 
 def exchange(tiles, farm_area, capacity, offsets, state):
@@ -384,12 +390,13 @@
             pltpu.VMEM((2, ROWS_X[1], 2 * LANES), f32),
             pltpu.VMEM((1, LANES), f32),
             pltpu.VMEM((1, LANES), f32),
-            pltpu.VMEM((128, 2, LANES), f32),
+            pltpu.VMEM((128, 1, LANES), f32),
+            pltpu.VMEM((128, 1, LANES), f32),
             pltpu.VMEM((M, QUADS, 16, LANES), bf16),
             dma((6,)), dma((8,)), dma((8,)), dma((8,)), dma((8,)),
             dma((2, 8)), dma((2, 8)), dma((8,)), dma((8,)),
             dma((2, 3)), dma((2, 3)), dma((3,)), dma((3,)),
-            dma, dma,
+            dma((2,)), dma((2,)),
         ],
         compiler_params=pltpu.CompilerParams(
             collective_id=0, has_side_effects=True, vmem_limit_bytes=60 * 2**20),

time: 36.5 us -> 37.1 us (1.016)
  Pallas kernels: 36.4 us -> 36.9 us
    pallas_call x1, Pallas kernels: 29.3 us -> 29.8 us  [exchange(): pl.pallas_call(exchange_kernel, out_shape=(pltpu.VMEM((M, AREAS), f32), p...]
where the time goes in v8:
time: 37.1 us; the launch traced here: 36.9 us
  Pallas kernels  36.9 us (99%)
    pallas_call x1, Pallas kernels, exchange(): pl.pallas_call(exchange_kernel, out_shape=(pltpu.VMEM((M, AREAS), f32), p...  29.8 us
    pallas_call x1, Pallas kernels, product(): pl.pallas_call(product_kernel, out_shape=jax.ShapeDtypeStruct((AREAS, QUA...  7.1 us

profile of v8, /device:TPU:1, one launch (start us, length us, event | category | flops | bytes accessed | tf_op | source)
XLA Modules:
  0.0 36.9 jit_solution(15747014719833600268)
XLA Ops:
  0.0 29.8 %exchange.1 = (f32[48,512]{1,0:T(8,128)S(1)}, bf16[8,192,512]{2,1,0:T(8,128)(2,1)S(1)}) custom-call(bf16[48,144,256]{2,1,0:T(8,128)(2,1)} %bitcast.13, s32[1,256]{1,0:T(1,128)} %bitcast.15, s32[1,256]{1,0:T(1,128)} %bitcast.16, s32[16]{0:T(128)} %offsets.1, bf16[48,8,16,128]{3,2,1,0:T(8,128)(2,1)} %bitcast.14), custom_call_target="tpu_custom_call" | custom-call | flops 536870912 | bytes 5242880 | tf_op jit(solution)/shard_map/exchange/pallas_call | solution.py:368
  29.8 7.1 %product.1 = bf16[512,8,16,128]{3,2,1,0:T(8,128)(2,1)} custom-call(f32[48,512]{1,0:T(8,128)S(1)} %get-tuple-element.7.metric, bf16[8,192,512]{2,1,0:T(8,128)(2,1)S(1)} %get-tuple-element.8.slab), custom_call_target="tpu_custom_call" | custom-call | flops 3221225472 | bytes 20971520 | tf_op jit(solution)/shard_map/product/pallas_call | solution.py:468

commit v9 on v7

--- a/solution.py
+++ b/solution.py
@@ -57,7 +57,7 @@
 
 def exchange_kernel(
     tiles, farm_area, capacity, offsets, state, metric_out, slab_out,
-    area_in, capacity_in, offsets_in,
+    area_in, capacity_in, offsets_in, near_tiles,
     facts_x, facts_z, got_x, got_z, weight_x, weight_z,
     part_x, part_z, sum_x, sum_z, near_x, off_x, off_z,
     metrics, st,
@@ -118,17 +118,21 @@
         return got_z.at[pl.ds(0, ROWS_Z), pl.ds(F * i, F)]
 
     def x_tile(xx, cc):
-        return tiles.at[12 * y + 2 * xx + cc]
+        return near_tiles.at[2 * xx + cc]
 
     def z_tile(zz, cc):
-        return tiles.at[12 * y + 8 + zz, pl.ds(pl.multiple_of(HALF * cc, HALF), ROWS_Z)]
+        return near_tiles.at[8 + zz, pl.ds(pl.multiple_of(HALF * cc, HALF), ROWS_Z)]
 
     local = [
         pltpu.make_async_copy(farm_area, area_in, local_sem.at[0]),
         pltpu.make_async_copy(capacity, capacity_in, local_sem.at[1]),
         pltpu.make_async_copy(offsets, offsets_in, local_sem.at[2]),
-        pltpu.make_async_copy(z_tile(z, c), z_slot(0), local_sem.at[3]),
-        pltpu.make_async_copy(x_tile(x, c), got_x.at[pl.ds(ONES, T), pl.ds(0, F)], local_sem.at[4]),
+        pltpu.make_async_copy(tiles.at[pl.ds(12 * y, 12)], near_tiles, local_sem.at[6]),
+        pltpu.make_async_copy(
+            tiles.at[12 * y + 8 + z, pl.ds(pl.multiple_of(HALF * c, HALF), ROWS_Z)],
+            z_slot(0), local_sem.at[3]),
+        pltpu.make_async_copy(
+            tiles.at[12 * y + mine_x], got_x.at[pl.ds(ONES, T), pl.ds(0, F)], local_sem.at[4]),
         pltpu.make_async_copy(state, st, local_sem.at[5]),
     ]
     for copy in local:
@@ -178,6 +182,7 @@
     pl.semaphore_wait(barrier, 16)
     for i in ORDER:
         start(fx_copy(i), fz_copy(i))
+    local[3].wait()
     for i in ORDER:
         start(x_copy(i, 0), z_copy(i))
     for i in ORDER[2:] + ORDER[:2]:
@@ -237,7 +242,7 @@
             sum_copy(half, rows, 1, zs[1]).start()
 
     early_rows, late_rows = pl.ds(0, 8 + ROWS_X[0]), pl.ds(8 + ROWS_X[0], ROWS_X[1])
-    local[4].wait()
+    local[5].wait()
     for i in range(1, 8):
         wait_for(x_slot(i, 0), x_send.at[0, i], x_recv.at[0, i])
 
@@ -245,7 +250,7 @@
     def _(p):
         leave(0, early_rows, p, dot_x(0, ONES + ROWS_X[0], p, pl.ds(0, 8 * F))[8:])
 
-    local[3].wait()
+    local[4].wait()
     for i in range(1, 8):
         wait_for(z_slot(i), z_send.at[i], z_recv.at[i])
     for h in range(2):
@@ -315,7 +320,7 @@
         xx, cc = x_peers[i]
         broadcast(xx, z, cc, y)
 
-    local[5].wait()
+    local[6].wait()
 
     @loop(0, QUADS)
     def _(i):
@@ -371,6 +376,7 @@
             pltpu.VMEM((1, F), jnp.int32),
             pltpu.VMEM((1, F), jnp.int32),
             pltpu.SMEM((16,), jnp.int32),
+            pltpu.VMEM((12, T, F), bf16),
             pltpu.VMEM((8, 4, F), f32),
             pltpu.VMEM((8, 4, F), f32),
             pltpu.VMEM((PAD_X, 8 * F), bf16),
@@ -386,7 +392,7 @@
             pltpu.VMEM((1, LANES), f32),
             pltpu.VMEM((128, 2, LANES), f32),
             pltpu.VMEM((M, QUADS, 16, LANES), bf16),
-            dma((6,)), dma((8,)), dma((8,)), dma((8,)), dma((8,)),
+            dma((7,)), dma((8,)), dma((8,)), dma((8,)), dma((8,)),
             dma((2, 8)), dma((2, 8)), dma((8,)), dma((8,)),
             dma((2, 3)), dma((2, 3)), dma((3,)), dma((3,)),
             dma, dma,

time: 36.5 us -> 36.3 us (level)
  no operation moved by 1% of the time
where the time goes in v9:
time: 36.3 us; the launch traced here: 36.2 us
  Pallas kernels  36.2 us (100%)
    pallas_call x1, Pallas kernels, exchange(): pl.pallas_call(exchange_kernel, out_shape=(pltpu.VMEM((M, AREAS), f32), p...  29.1 us
    pallas_call x1, Pallas kernels, product(): pl.pallas_call(product_kernel, out_shape=jax.ShapeDtypeStruct((AREAS, QUA...  7.1 us

profile of v9, /device:TPU:1, one launch (start us, length us, event | category | flops | bytes accessed | tf_op | source)
XLA Modules:
  0.0 36.2 jit_solution(5976393191119972188)
XLA Ops:
  0.0 29.1 %exchange.1 = (f32[48,512]{1,0:T(8,128)S(1)}, bf16[8,192,512]{2,1,0:T(8,128)(2,1)S(1)}) custom-call(bf16[48,144,256]{2,1,0:T(8,128)(2,1)} %bitcast.13, s32[1,256]{1,0:T(1,128)} %bitcast.15, s32[1,256]{1,0:T(1,128)} %bitcast.16, s32[16]{0:T(128)} %offsets.1, bf16[48,8,16,128]{3,2,1,0:T(8,128)(2,1)} %bitcast.14), custom_call_target="tpu_custom_call" | custom-call | flops 536870912 | bytes 5242880 | tf_op jit(solution)/shard_map/exchange/pallas_call | solution.py:367
  29.1 7.1 %product.1 = bf16[512,8,16,128]{3,2,1,0:T(8,128)(2,1)} custom-call(f32[48,512]{1,0:T(8,128)S(1)} %get-tuple-element.7.metric, bf16[8,192,512]{2,1,0:T(8,128)(2,1)S(1)} %get-tuple-element.8.slab), custom_call_target="tpu_custom_call" | custom-call | flops 3221225472 | bytes 20971520 | tf_op jit(solution)/shard_map/product/pallas_call | solution.py:467

commit v10 on v9

--- a/solution.py
+++ b/solution.py
@@ -52,13 +52,13 @@
 BACK = (0, 1, 4, 5, 2, 3, 6, 7)
 ORDER = (6, 7, 2, 4, 3, 5, 1)
 NEAR = 6
-STARTS, ROWS_X = (0, 96), (96, 48)
+STARTS, ROWS_X, SKIP = (0, 96), (96, 48), (ONES, 0)
 
 
 def exchange_kernel(
     tiles, farm_area, capacity, offsets, state, metric_out, slab_out,
     area_in, capacity_in, offsets_in, near_tiles,
-    facts_x, facts_z, got_x, got_z, weight_x, weight_z,
+    facts_x, facts_z, got_a, got_b, got_z, weight_x, weight_z,
     part_x, part_z, sum_x, sum_z, near_x, off_x, off_z,
     metrics, st,
     local_sem, fx_send, fx_recv, fz_send, fz_recv, x_send, x_recv, z_send, z_recv,
@@ -97,6 +97,7 @@
             lax.fori_loop(first, last, lambda i, carry: (body(i), carry)[1], 0)
         return run
 
+    got_x = (got_a, got_b)
     barrier = pltpu.get_barrier_semaphore()
 
     def greet(to):
@@ -112,10 +113,10 @@
         greet(device(x, z, c, ys[d]))
 
     def x_slot(i, half):
-        return got_x.at[pl.ds(ONES + STARTS[half], ROWS_X[half]), pl.ds(F * i, F)]
+        return got_x[half].at[i, pl.ds(SKIP[half], ROWS_X[half])]
 
     def z_slot(i):
-        return got_z.at[pl.ds(0, ROWS_Z), pl.ds(F * i, F)]
+        return got_z.at[i, pl.ds(0, ROWS_Z)]
 
     def x_tile(xx, cc):
         return near_tiles.at[2 * xx + cc]
@@ -132,7 +133,11 @@
             tiles.at[12 * y + 8 + z, pl.ds(pl.multiple_of(HALF * c, HALF), ROWS_Z)],
             z_slot(0), local_sem.at[3]),
         pltpu.make_async_copy(
-            tiles.at[12 * y + mine_x], got_x.at[pl.ds(ONES, T), pl.ds(0, F)], local_sem.at[4]),
+            tiles.at[12 * y + mine_x, pl.ds(STARTS[0], ROWS_X[0])], x_slot(0, 0),
+            local_sem.at[4]),
+        pltpu.make_async_copy(
+            tiles.at[12 * y + mine_x, pl.ds(STARTS[1], ROWS_X[1])], x_slot(0, 1),
+            local_sem.at[7]),
         pltpu.make_async_copy(state, st, local_sem.at[5]),
     ]
     for copy in local:
@@ -188,8 +193,8 @@
     for i in ORDER[2:] + ORDER[:2]:
         start(x_copy(i, 1))
 
-    got_x[pl.ds(0, ONES)] = jnp.ones((ONES, 8 * F), jnp.bfloat16)
-    got_z[pl.ds(ROWS_Z, 16)] = jnp.ones((16, 8 * F), jnp.bfloat16)
+    got_a[:, pl.ds(0, ONES)] = jnp.ones((8, ONES, F), jnp.bfloat16)
+    got_z[:, pl.ds(ROWS_Z, ONES)] = jnp.ones((8, ONES, F), jnp.bfloat16)
     off_x[...] = jnp.zeros_like(off_x)
     off_z[...] = jnp.zeros_like(off_z)
     area_ids = iota((AREAS, F), 0).astype(jnp.float32)
@@ -217,16 +222,20 @@
 
     bz = []
 
-    near, far = pl.ds(0, NEAR * F), pl.ds(NEAR * F, (8 - NEAR) * F)
+    near, far, all_slots = range(NEAR), range(NEAR, 8), range(8)
 
     def block_pair(p):
         return lax.rem(z + 2 + p, 4), lax.rem(z + 1 + 3 * p, 4)
 
-    def dot_x(first, count, p, columns):
+    def side_by_side(got, slots):
+        return jnp.concatenate([got[i] for i in slots], axis=1)
+
+    def dot_x(half, p, slots):
+        columns = pl.ds(F * slots[0], F * len(slots))
         chosen = jnp.concatenate(
             [weight_x[pl.ds(pl.multiple_of(LANES * zz, LANES), LANES), columns]
              for zz in block_pair(p)], axis=0)
-        return sum_up(got_x[pl.ds(first, count), columns], chosen)
+        return sum_up(side_by_side(got_x[half], slots), chosen)
 
     def sum_copy(half, rows, d, zz):
         return remote(part_x.at[zz, rows], sum_x.at[3 - d, rows], bx_send.at[half, d - 1],
@@ -248,13 +257,13 @@
 
     @loop(0, 2)
     def _(p):
-        leave(0, early_rows, p, dot_x(0, ONES + ROWS_X[0], p, pl.ds(0, 8 * F))[8:])
+        leave(0, early_rows, p, dot_x(0, p, all_slots)[8:])
 
     local[4].wait()
     for i in range(1, 8):
         wait_for(z_slot(i), z_send.at[i], z_recv.at[i])
     for h in range(2):
-        value = sum_up(got_z[...], weight_z[pl.ds(2 * LANES * h, 2 * LANES)])
+        value = sum_up(side_by_side(got_z, all_slots), weight_z[pl.ds(2 * LANES * h, 2 * LANES)])
         for b in range(2):
             part_z[2 * h + b] = value[:KEEP_Z, b * LANES : (b + 1) * LANES]
     for d in (2, 1, 3):
@@ -263,19 +272,20 @@
         copy.start()
         bz.append(copy)
 
+    local[6].wait()
     for i in range(1, NEAR):
         wait_for(x_slot(i, 1), x_send.at[1, i], x_recv.at[1, i])
 
     @loop(0, 2)
     def _(p):
-        near_x[p] = dot_x(ONES + ROWS_X[0], ROWS_X[1], p, near)
+        near_x[p] = dot_x(1, p, near)
 
     for i in range(NEAR, 8):
         wait_for(x_slot(i, 1), x_send.at[1, i], x_recv.at[1, i])
 
     @loop(0, 2)
     def _(p):
-        leave(1, late_rows, p, near_x[p] + dot_x(ONES + ROWS_X[0], ROWS_X[1], p, far))
+        leave(1, late_rows, p, near_x[p] + dot_x(1, p, far))
 
     bx = [[sum_copy(half, rows, d, zs[d]) for d in range(1, 4)]
           for half, rows in ((0, early_rows), (1, late_rows))]
@@ -320,7 +330,7 @@
         xx, cc = x_peers[i]
         broadcast(xx, z, cc, y)
 
-    local[6].wait()
+    local[7].wait()
 
     @loop(0, QUADS)
     def _(i):
@@ -379,8 +389,9 @@
             pltpu.VMEM((12, T, F), bf16),
             pltpu.VMEM((8, 4, F), f32),
             pltpu.VMEM((8, 4, F), f32),
-            pltpu.VMEM((PAD_X, 8 * F), bf16),
-            pltpu.VMEM((PAD_Z, 8 * F), bf16),
+            pltpu.VMEM((8, ONES + ROWS_X[0], F), bf16),
+            pltpu.VMEM((8, ROWS_X[1], F), bf16),
+            pltpu.VMEM((8, ROWS_Z + ONES, F), bf16),
             pltpu.VMEM((AREAS, 8 * F), bf16),
             pltpu.VMEM((AREAS, 8 * F), bf16),
             pltpu.VMEM((RING, KEEP_X, LANES), f32),
@@ -392,7 +403,7 @@
             pltpu.VMEM((1, LANES), f32),
             pltpu.VMEM((128, 2, LANES), f32),
             pltpu.VMEM((M, QUADS, 16, LANES), bf16),
-            dma((7,)), dma((8,)), dma((8,)), dma((8,)), dma((8,)),
+            dma((8,)), dma((8,)), dma((8,)), dma((8,)), dma((8,)),
             dma((2, 8)), dma((2, 8)), dma((8,)), dma((8,)),
             dma((2, 3)), dma((2, 3)), dma((3,)), dma((3,)),
             dma, dma,

time: 36.3 us -> 36.3 us (level)
  no operation moved by 1% of the time
where the time goes in v10:
time: 36.3 us; the launch traced here: 36.2 us
  Pallas kernels  36.2 us (100%)
    pallas_call x1, Pallas kernels, exchange(): pl.pallas_call(exchange_kernel, out_shape=(pltpu.VMEM((M, AREAS), f32), p...  29.1 us
    pallas_call x1, Pallas kernels, product(): pl.pallas_call(product_kernel, out_shape=jax.ShapeDtypeStruct((AREAS, QUA...  7.1 us

profile of v10, /device:TPU:1, one launch (start us, length us, event | category | flops | bytes accessed | tf_op | source)
XLA Modules:
  0.0 36.2 jit_solution(8112165137093608247)
XLA Ops:
  0.0 29.1 %exchange.1 = (f32[48,512]{1,0:T(8,128)S(1)}, bf16[8,192,512]{2,1,0:T(8,128)(2,1)S(1)}) custom-call(bf16[48,144,256]{2,1,0:T(8,128)(2,1)} %bitcast.13, s32[1,256]{1,0:T(1,128)} %bitcast.15, s32[1,256]{1,0:T(1,128)} %bitcast.16, s32[16]{0:T(128)} %offsets.1, bf16[48,8,16,128]{3,2,1,0:T(8,128)(2,1)} %bitcast.14), custom_call_target="tpu_custom_call" | custom-call | flops 536870912 | bytes 5242880 | tf_op jit(solution)/shard_map/exchange/pallas_call | solution.py:377
  29.1 7.1 %product.1 = bf16[512,8,16,128]{3,2,1,0:T(8,128)(2,1)} custom-call(f32[48,512]{1,0:T(8,128)S(1)} %get-tuple-element.7.metric, bf16[8,192,512]{2,1,0:T(8,128)(2,1)S(1)} %get-tuple-element.8.slab), custom_call_target="tpu_custom_call" | custom-call | flops 3221225472 | bytes 20971520 | tf_op jit(solution)/shard_map/product/pallas_call | solution.py:478

commit v11 on v10

--- a/solution.py
+++ b/solution.py
@@ -315,20 +315,14 @@
 
     mine = metrics.at[spot]
 
-    def broadcast(xx, zz, cc, yy):
-        remote(mine, mine, all_send, all_recv, device(xx, zz, cc, yy)).start()
-
-    @loop(0, 15)
-    def _(k):
-        step = 1 + lax.rem(k + 9, 15)
-        yy, zz = lax.rem(y + lax.div(step, 4), 4), lax.rem(z + lax.rem(step, 4), 4)
-        for i in (6, 7, 2, 3, 4, 5, 0, 1):
-            xx, cc = x_peers[i]
-            broadcast(xx, zz, cc, yy)
-
-    for i in ORDER:
+    def hops(where):
+        dy, dz, i = where
+        return sum(min(d, 4 - d) for d in (dy, dz, STEP[i]))
+
+    others = [(dy, dz, i) for dy in range(4) for dz in range(4) for i in range(8)][1:]
+    for dy, dz, i in sorted(others, key=hops, reverse=True):
         xx, cc = x_peers[i]
-        broadcast(xx, z, cc, y)
+        remote(mine, mine, all_send, all_recv, device(xx, zs[dz], cc, ys[dy])).start()
 
     local[7].wait()
 

time: 36.3 us -> 35.3 us (0.972)
  Pallas kernels: 36.2 us -> 35.2 us
    pallas_call x1, Pallas kernels: 29.1 us -> 28.1 us  [exchange(): pl.pallas_call(exchange_kernel, out_shape=(pltpu.VMEM((M, AREAS), f32), p...]
where the time goes in v11:
time: 35.3 us; the launch traced here: 35.2 us
  Pallas kernels  35.2 us (100%)
    pallas_call x1, Pallas kernels, exchange(): pl.pallas_call(exchange_kernel, out_shape=(pltpu.VMEM((M, AREAS), f32), p...  28.1 us
    pallas_call x1, Pallas kernels, product(): pl.pallas_call(product_kernel, out_shape=jax.ShapeDtypeStruct((AREAS, QUA...  7.1 us

profile of v11, /device:TPU:1, one launch (start us, length us, event | category | flops | bytes accessed | tf_op | source)
XLA Modules:
  0.0 35.2 jit_solution(4347751756804059366)
XLA Ops:
  0.0 28.1 %exchange.1 = (f32[48,512]{1,0:T(8,128)S(1)}, bf16[8,192,512]{2,1,0:T(8,128)(2,1)S(1)}) custom-call(bf16[48,144,256]{2,1,0:T(8,128)(2,1)} %bitcast.13, s32[1,256]{1,0:T(1,128)} %bitcast.15, s32[1,256]{1,0:T(1,128)} %bitcast.16, s32[16]{0:T(128)} %offsets.1, bf16[48,8,16,128]{3,2,1,0:T(8,128)(2,1)} %bitcast.14), custom_call_target="tpu_custom_call" | custom-call | flops 536870912 | bytes 5242880 | tf_op jit(solution)/shard_map/exchange/pallas_call | solution.py:371
  28.1 7.1 %product.1 = bf16[512,8,16,128]{3,2,1,0:T(8,128)(2,1)} custom-call(f32[48,512]{1,0:T(8,128)S(1)} %get-tuple-element.7.metric, bf16[8,192,512]{2,1,0:T(8,128)(2,1)S(1)} %get-tuple-element.8.slab), custom_call_target="tpu_custom_call" | custom-call | flops 3221225472 | bytes 20971520 | tf_op jit(solution)/shard_map/product/pallas_call | solution.py:472

commit v12 on v11

--- a/solution.py
+++ b/solution.py
@@ -140,7 +140,7 @@
             local_sem.at[7]),
         pltpu.make_async_copy(state, st, local_sem.at[5]),
     ]
-    for copy in local:
+    for copy in local[:4]:
         copy.start()
     def fx_copy(i):
         xx, cc = x_peers[i]
@@ -192,6 +192,8 @@
         start(x_copy(i, 0), z_copy(i))
     for i in ORDER[2:] + ORDER[:2]:
         start(x_copy(i, 1))
+    for copy in local[4:]:
+        copy.start()
 
     got_a[:, pl.ds(0, ONES)] = jnp.ones((8, ONES, F), jnp.bfloat16)
     got_z[:, pl.ds(ROWS_Z, ONES)] = jnp.ones((8, ONES, F), jnp.bfloat16)

time: 35.3 us -> 35.3 us (level)
  no operation moved by 1% of the time
where the time goes in v12:
time: 35.3 us; the launch traced here: 35.2 us
  Pallas kernels  35.2 us (100%)
    pallas_call x1, Pallas kernels, exchange(): pl.pallas_call(exchange_kernel, out_shape=(pltpu.VMEM((M, AREAS), f32), p...  28.1 us
    pallas_call x1, Pallas kernels, product(): pl.pallas_call(product_kernel, out_shape=jax.ShapeDtypeStruct((AREAS, QUA...  7.1 us

profile of v12, /device:TPU:1, one launch (start us, length us, event | category | flops | bytes accessed | tf_op | source)
XLA Modules:
  0.0 35.2 jit_solution(15943482909928172537)
XLA Ops:
  0.0 28.1 %exchange.1 = (f32[48,512]{1,0:T(8,128)S(1)}, bf16[8,192,512]{2,1,0:T(8,128)(2,1)S(1)}) custom-call(bf16[48,144,256]{2,1,0:T(8,128)(2,1)} %bitcast.13, s32[1,256]{1,0:T(1,128)} %bitcast.15, s32[1,256]{1,0:T(1,128)} %bitcast.16, s32[16]{0:T(128)} %offsets.1, bf16[48,8,16,128]{3,2,1,0:T(8,128)(2,1)} %bitcast.14), custom_call_target="tpu_custom_call" | custom-call | flops 536870912 | bytes 5242880 | tf_op jit(solution)/shard_map/exchange/pallas_call | solution.py:373
  28.1 7.1 %product.1 = bf16[512,8,16,128]{3,2,1,0:T(8,128)(2,1)} custom-call(f32[48,512]{1,0:T(8,128)S(1)} %get-tuple-element.7.metric, bf16[8,192,512]{2,1,0:T(8,128)(2,1)S(1)} %get-tuple-element.8.slab), custom_call_target="tpu_custom_call" | custom-call | flops 3221225472 | bytes 20971520 | tf_op jit(solution)/shard_map/product/pallas_call | solution.py:474

commit v13 on v12

--- a/solution.py
+++ b/solution.py
@@ -438,24 +438,30 @@
         some = pl.ds(pl.multiple_of(2 * areas * q, 2 * areas), 2 * areas)
         return pltpu.make_async_copy(stage.at[some, i], out.at[some, i], out_sem.at[QUADS * q + i])
 
+    def make(q, slot):
+        for r in range(2):
+            rows = pl.ds(pl.multiple_of((2 * q + r) * areas, areas), areas)
+            repeated = jnp.dot(repeat, wide[rows], preferred_element_type=jnp.float32)
+            lhs[slot, r] = jnp.where(keep, repeated, 0.0).astype(jnp.bfloat16)
+
+    make(0, 0)
+
     def step(q, carry):
         first = [pl.multiple_of((2 * q + r) * areas, areas) for r in range(2)]
-        for r in range(2):
-            rows = jnp.dot(repeat, wide[pl.ds(first[r], areas)],
-                           preferred_element_type=jnp.float32)
-            lhs[r] = jnp.where(keep, rows, 0.0).astype(jnp.bfloat16)
+        slot = q & 1
         for i in range(QUADS):
             for r in range(2):
                 parts = []
                 for h in range(2):
-                    acc = jnp.dot(lhs[r], slab[i, :, pl.ds(2 * LANES * h, 2 * LANES)],
+                    acc = jnp.dot(lhs[slot, r], slab[i, :, pl.ds(2 * LANES * h, 2 * LANES)],
                                   preferred_element_type=jnp.float32)
                     acc = (acc * (1.0 / (M - 1))).reshape(ROWS // 8, 8, 2 * LANES)
                     both = swap_halves(acc[:, :, :LANES], acc[:, :, LANES:])
                     parts.append(jnp.stack(both, axis=1).reshape(areas, 8, LANES))
                 done = jnp.stack(parts, axis=1).reshape(areas, 16, LANES)
                 stage[pl.ds(first[r], areas), i] = done.astype(jnp.bfloat16)
-            part(q, i).start(priority=i % 2)
+            part(q, i).start()
+        make((q + 1) & 3, 1 - slot)
         return carry
 
     lax.fori_loop(0, half, step, 0)
@@ -478,7 +484,7 @@
         out_specs=any_space,
         scratch_shapes=[
             pltpu.VMEM((AREAS, 4 * M), jnp.bfloat16),
-            pltpu.VMEM((2, ROWS, 4 * M), jnp.bfloat16),
+            pltpu.VMEM((2, 2, ROWS, 4 * M), jnp.bfloat16),
             pltpu.VMEM((AREAS, QUADS, 16, LANES), jnp.bfloat16),
             dma((32,)),
         ],

time: 35.3 us -> 35.2 us (level)
  no operation moved by 1% of the time
where the time goes in v13:
time: 35.2 us; the launch traced here: 35.1 us
  Pallas kernels  35.1 us (100%)
    pallas_call x1, Pallas kernels, exchange(): pl.pallas_call(exchange_kernel, out_shape=(pltpu.VMEM((M, AREAS), f32), p...  28.1 us
    pallas_call x1, Pallas kernels, product(): pl.pallas_call(product_kernel, out_shape=jax.ShapeDtypeStruct((AREAS, QUA...  6.99 us

profile of v13, /device:TPU:1, one launch (start us, length us, event | category | flops | bytes accessed | tf_op | source)
XLA Modules:
  0.0 35.1 jit_solution(10540017701353484685)
XLA Ops:
  0.0 28.1 %exchange.1 = (f32[48,512]{1,0:T(8,128)S(1)}, bf16[8,192,512]{2,1,0:T(8,128)(2,1)S(1)}) custom-call(bf16[48,144,256]{2,1,0:T(8,128)(2,1)} %bitcast.13, s32[1,256]{1,0:T(1,128)} %bitcast.15, s32[1,256]{1,0:T(1,128)} %bitcast.16, s32[16]{0:T(128)} %offsets.1, bf16[48,8,16,128]{3,2,1,0:T(8,128)(2,1)} %bitcast.14), custom_call_target="tpu_custom_call" | custom-call | flops 536870912 | bytes 5242880 | tf_op jit(solution)/shard_map/exchange/pallas_call | solution.py:373
  28.1 7.0 %product.1 = bf16[512,8,16,128]{3,2,1,0:T(8,128)(2,1)} custom-call(f32[48,512]{1,0:T(8,128)S(1)} %get-tuple-element.7.metric, bf16[8,192,512]{2,1,0:T(8,128)(2,1)S(1)} %get-tuple-element.8.slab), custom_call_target="tpu_custom_call" | custom-call | flops 3221225472 | bytes 20971520 | tf_op jit(solution)/shard_map/product/pallas_call | solution.py:480

commit v14 on v13

--- a/solution.py
+++ b/solution.py
@@ -180,8 +180,7 @@
     turned = ((area >> 5) & 3) * 128 + (area >> 7) * 32 + (area & 31)
     for facts, ids, spot in ((facts_z, turned, mine_z), (facts_x, area, mine_x)):
         placed = jnp.where((lane >> 4) == spot, offset, 0)
-        rows = jnp.concatenate(
-            [ids, capacity_in[...], placed, jnp.zeros((1, F), jnp.int32)], axis=0)
+        rows = jnp.concatenate([ids, capacity_in[...] + 256 * placed], axis=0)
         facts[0] = rows.astype(jnp.float32)
 
     pl.semaphore_wait(barrier, 16)
@@ -203,8 +202,9 @@
 
     def weigh(i, facts, weight, off):
         rows = facts[i]
-        off[...] = off[...] + rows[2:3, :LANES]
-        placed = jnp.where(area_ids == rows[0:1], rows[1:2], 0.0)
+        shift = jnp.floor(rows[1:2] * (1 / 256))
+        off[...] = off[...] + shift[:, :LANES]
+        placed = jnp.where(area_ids == rows[0:1], rows[1:2] - 256 * shift, 0.0)
         weight[:, pl.ds(pl.multiple_of(F * i, F), F)] = placed.astype(jnp.bfloat16)
 
     @loop(0, 8)
@@ -383,8 +383,8 @@
             pltpu.VMEM((1, F), jnp.int32),
             pltpu.SMEM((16,), jnp.int32),
             pltpu.VMEM((12, T, F), bf16),
-            pltpu.VMEM((8, 4, F), f32),
-            pltpu.VMEM((8, 4, F), f32),
+            pltpu.VMEM((8, 2, F), f32),
+            pltpu.VMEM((8, 2, F), f32),
             pltpu.VMEM((8, ONES + ROWS_X[0], F), bf16),
             pltpu.VMEM((8, ROWS_X[1], F), bf16),
             pltpu.VMEM((8, ROWS_Z + ONES, F), bf16),

time: 35.2 us -> 35 us (level)
  no operation moved by 1% of the time
where the time goes in v14:
time: 35 us; the launch traced here: 34.9 us
  Pallas kernels  34.9 us (100%)
    pallas_call x1, Pallas kernels, exchange(): pl.pallas_call(exchange_kernel, out_shape=(pltpu.VMEM((M, AREAS), f32), p...  27.9 us
    pallas_call x1, Pallas kernels, product(): pl.pallas_call(product_kernel, out_shape=jax.ShapeDtypeStruct((AREAS, QUA...  6.99 us

profile of v14, /device:TPU:1, one launch (start us, length us, event | category | flops | bytes accessed | tf_op | source)
XLA Modules:
  0.0 34.9 jit_solution(9385269261464710700)
XLA Ops:
  0.0 27.9 %exchange.1 = (f32[48,512]{1,0:T(8,128)S(1)}, bf16[8,192,512]{2,1,0:T(8,128)(2,1)S(1)}) custom-call(bf16[48,144,256]{2,1,0:T(8,128)(2,1)} %bitcast.13, s32[1,256]{1,0:T(1,128)} %bitcast.15, s32[1,256]{1,0:T(1,128)} %bitcast.16, s32[16]{0:T(128)} %offsets.1, bf16[48,8,16,128]{3,2,1,0:T(8,128)(2,1)} %bitcast.14), custom_call_target="tpu_custom_call" | custom-call | flops 536870912 | bytes 5242880 | tf_op jit(solution)/shard_map/exchange/pallas_call | solution.py:373
  27.9 7.0 %product.1 = bf16[512,8,16,128]{3,2,1,0:T(8,128)(2,1)} custom-call(f32[48,512]{1,0:T(8,128)S(1)} %get-tuple-element.7.metric, bf16[8,192,512]{2,1,0:T(8,128)(2,1)S(1)} %get-tuple-element.8.slab), custom_call_target="tpu_custom_call" | custom-call | flops 3221225472 | bytes 20971520 | tf_op jit(solution)/shard_map/product/pallas_call | solution.py:480
